TPU v7x, 512 devices: a whole 4x4x16 slice. The times are simulated.
512 devices in a mesh: blk: 32 (over x, y, core), tile: 16 (over z).
Axes of the slice: x: 4, y: 4, z: 16, core: 2. Of those that a mesh axis runs over, the one named last changes fastest.
Arguments:
- field: bfloat16 [32, 16, 1024, 128], P('blk', 'tile'), may hold values from -6 to 6
- grid_cotangent: bfloat16 [32, 16, 2048, 128], P('blk', 'tile'), may hold values from -6 to 6
- send_rows: int32 [32, 16, 4, 256], P('blk', 'tile'), may hold values from 0 to 1023
- neighbors: int32 [32, 16, 1024, 8], P('blk', 'tile'), may hold values from 0 to 2047
- stencil: float32 [32, 16, 1024, 8], P('blk', 'tile'), may hold values from -2.5 to 2.5
- vertical: float32 [2, 16, 16], replicated, may hold values from -1.5 to 1.5
- interp_weights: bfloat16 [32, 16, 16, 128, 128], P('blk', 'tile'), may hold values from -0.5 to 0.5
- block_map: int32 [32, 16, 16, 128], P('blk', 'tile'), may hold values from 0 to 1023
- live_block_tally: int32 [32, 16], P('blk', 'tile'), may hold values from 2 to 16, as said below
Outputs:
- grid_field: bfloat16 [32, 16, 2048, 128], P('blk', 'tile')
- subgrid_gradient: bfloat16 [32, 16, 1024, 128], P('blk', 'tile')
Inputs may be any that keep to these rules, and one draw needn't show every extreme that they name: `live_block_tally`: each device's count is one of 16, 8, 4, 2; at least one device has 16.
All inputs are finite; a program needn't handle non-finite values.
Results may differ from a plain program's by a relative error of at most 0.017.
Values may be sent and summed in bfloat16 or wider, within the bound.
No kernel may reach another device: no remote copies, remote signals or barrier semaphores. Data moves between devices by JAX's collectives and lax.ppermute only.
A program may use at most 64 MiB of HBM per device.

v0:
```python
import jax
import jax.numpy as jnp
from jax import lax
from jax.sharding import PartitionSpec as P

MEMBERS = 4


def from_behind(value, axis, steps):
    count = lax.axis_size(axis)
    pairs = [(source, (source + steps) % count) for source in range(count)]
    return lax.ppermute(value, axis, pairs)


def shifted(value, axis, steps):
    count = lax.axis_size(axis)
    first, last = (max(0, -steps), min(count, count - steps))
    return lax.ppermute(value, axis, [(source, source + steps) for source in range(first, last)])


def level_matrix(vertical, member_list):
    variable_count = vertical.shape[0]
    level_count = vertical.shape[1]
    member_identity = jnp.eye(member_list, dtype=jnp.float32)
    variable_identity = jnp.eye(variable_count, dtype=jnp.float32)
    block_stack = jnp.einsum("ec,yf,yhs->eyhcfs", member_identity, variable_identity, vertical)
    width = member_list * variable_count * level_count
    return block_stack.reshape(width, width)


def split_pair(values):
    high = values.astype(jnp.bfloat16)
    low = (values - high.astype(jnp.float32)).astype(jnp.bfloat16)
    return (high, low)


def lead_dot(left, right):
    return lax.dot_general(
        left, right, (((0,), (0,)), ((), ())), preferred_element_type=jnp.float32
    )


def one_hot_rows(indices, width):
    columns = jnp.arange(width, dtype=jnp.int32)
    return (indices[..., None] == columns).astype(jnp.bfloat16)


def stencil_matrix(adjacent_part, coeff_part, width):
    columns = jnp.arange(width, dtype=jnp.int32)
    total = jnp.zeros((adjacent_part.shape[0], width), jnp.float32)
    for k in range(adjacent_part.shape[1]):
        total = total + jnp.where(
            adjacent_part[:, k : k + 1] == columns, coeff_part[:, k : k + 1], 0.0
        )
    return total


def row_blocks(values, rows_each):
    return values.reshape((values.shape[0] // rows_each, rows_each) + values.shape[1:])


def forward_local(extended, adjacent, coeffs, mixing, weight_table, block_rows, live_count):
    feat = extended.shape[1]
    own_rows = adjacent.shape[0]
    width = extended.shape[0]
    rows_each = min(512, own_rows)

    def convolve(items):
        adjacent_part, coeff_part = items
        high, low = split_pair(stencil_matrix(adjacent_part, coeff_part, width))
        return jnp.dot(high, extended, preferred_element_type=jnp.float32) + jnp.dot(
            low, extended, preferred_element_type=jnp.float32
        )

    horizontal = lax.map(convolve, (row_blocks(adjacent, rows_each), row_blocks(coeffs, rows_each)))
    horizontal = horizontal.reshape(own_rows, feat)
    converted = jnp.dot(
        horizontal, mixing, precision=lax.Precision.HIGHEST, preferred_element_type=jnp.float32
    ).astype(jnp.bfloat16)
    slots = weight_table.shape[0]
    block = weight_table.shape[1]
    group = 4
    slot_ids = jnp.arange(slots, dtype=jnp.int32).reshape(slots // group, group)

    def place_group(items):
        weight_group, index_group, id_group = items
        source = jnp.einsum(
            "jsp,pf->jsf",
            one_hot_rows(index_group, own_rows),
            converted,
            preferred_element_type=jnp.float32,
        ).astype(jnp.bfloat16)
        result = jnp.einsum(
            "jrs,jsf->jrf", weight_group, source, preferred_element_type=jnp.float32
        )
        live = (id_group < live_count)[:, None, None]
        return jnp.where(live, result, 0.0).astype(jnp.bfloat16)

    grid = lax.map(
        place_group, (row_blocks(weight_table, group), row_blocks(block_rows, group), slot_ids)
    )
    return grid.reshape(slots * block, feat)


def adjoint_local(
    cotangent, weight_table, block_rows, live_count, mixing, adjacent, coeffs, halo_size
):
    slots = weight_table.shape[0]
    block = weight_table.shape[1]
    feat = cotangent.shape[1]
    own_rows = adjacent.shape[0]
    cot_blocks = cotangent.reshape(slots, block, feat)
    group = 4
    slot_ids = jnp.arange(slots, dtype=jnp.int32).reshape(slots // group, group)

    def gather_group(accum, items):
        weight_group, index_group, cot_group, id_group = items
        live = (id_group < live_count)[:, None, None]
        masked = jnp.where(live, cot_group, jnp.zeros_like(cot_group))
        result = jnp.einsum(
            "jrs,jrf->jsf", weight_group, masked, preferred_element_type=jnp.float32
        )
        high, low = split_pair(result)
        selector = one_hot_rows(index_group, own_rows)
        accum = accum + jnp.einsum(
            "jsp,jsf->pf", selector, high, preferred_element_type=jnp.float32
        )
        accum = accum + jnp.einsum("jsp,jsf->pf", selector, low, preferred_element_type=jnp.float32)
        return (accum, None)

    back, _ = lax.scan(
        gather_group,
        jnp.zeros((own_rows, feat), jnp.float32),
        (
            row_blocks(weight_table, group),
            row_blocks(block_rows, group),
            row_blocks(cot_blocks, group),
            slot_ids,
        ),
    )
    mixed_back = jnp.dot(
        back, mixing.T, precision=lax.Precision.HIGHEST, preferred_element_type=jnp.float32
    )
    width = own_rows + 4 * halo_size
    rows_each = min(512, own_rows)

    def spread(accum, items):
        adjacent_part, coeff_part, mixed_part = items
        weight_high, weight_low = split_pair(stencil_matrix(adjacent_part, coeff_part, width))
        mixed_high, mixed_low = split_pair(mixed_part)
        accum = accum + lead_dot(weight_high, mixed_high) + lead_dot(weight_high, mixed_low)
        accum = accum + lead_dot(weight_low, mixed_high)
        return (accum, None)

    adjoint_extended, _ = lax.scan(
        spread,
        jnp.zeros((width, feat), jnp.float32),
        (
            row_blocks(adjacent, rows_each),
            row_blocks(coeffs, rows_each),
            row_blocks(mixed_back, rows_each),
        ),
    )
    halo_back = adjoint_extended[own_rows:].astype(jnp.bfloat16).reshape(4, halo_size, feat)
    return (adjoint_extended[:own_rows], halo_back)


def shards(
    field,
    grid_cotangent,
    send_rows,
    neighbors,
    stencil,
    vertical,
    interp_weights,
    block_map,
    live_block_tally,
):
    local_rows = field[0, 0]
    send_lists = send_rows[0, 0]
    adjacent = neighbors[0, 0]
    coeffs = stencil[0, 0]
    weight_table = interp_weights[0, 0]
    block_rows = block_map[0, 0]
    live_count = live_block_tally[0, 0]
    cotangent = grid_cotangent[0, 0]
    halo_size = send_lists.shape[1]
    own_rows = local_rows.shape[0]
    feat = local_rows.shape[1]
    mixing = level_matrix(vertical, MEMBERS)
    send_selector = one_hot_rows(send_lists.reshape(-1), own_rows)
    picked = jnp.dot(send_selector, local_rows, preferred_element_type=jnp.float32).astype(
        jnp.bfloat16
    )
    picked = picked.reshape(4, halo_size, feat)
    outgoing = [picked[q] for q in range(4)]
    received = [None, None, None, None]
    returned = [None, None, None, None]
    for offset, sent in ((1, 0), (-1, 1)):
        received[sent] = from_behind(outgoing[sent], "blk", offset)
    for offset, sent in ((1, 2), (-1, 3)):
        received[sent] = shifted(outgoing[sent], "tile", offset)
    extended = jnp.concatenate([local_rows] + received, axis=0)
    grid = forward_local(extended, adjacent, coeffs, mixing, weight_table, block_rows, live_count)
    owned_portion, halo_back = adjoint_local(
        cotangent, weight_table, block_rows, live_count, mixing, adjacent, coeffs, halo_size
    )
    for offset, back_block in ((-1, 0), (1, 1)):
        returned[back_block] = from_behind(halo_back[back_block], "blk", offset)
    for offset, back_block in ((-1, 2), (1, 3)):
        returned[back_block] = shifted(halo_back[back_block], "tile", offset)
    returned_stack = jnp.concatenate(returned, axis=0)
    gradient = owned_portion + lead_dot(send_selector, returned_stack)
    return (grid[None, None], gradient.astype(jnp.bfloat16)[None, None])


def solution(mesh):
    in_specs = (
        P("blk", "tile", None, None),
        P("blk", "tile", None, None),
        P("blk", "tile", None, None),
        P("blk", "tile", None, None),
        P("blk", "tile", None, None),
        P(),
        P("blk", "tile", None, None, None),
        P("blk", "tile", None, None),
        P("blk", "tile"),
    )
    out_specs = (P("blk", "tile", None, None), P("blk", "tile", None, None))
    return jax.shard_map(shards, mesh=mesh, in_specs=in_specs, out_specs=out_specs, check_vma=False)
```

profile of v0, /device:TPU:96, one launch (start us, length us, event | category | flops | bytes accessed | tf_op | source)
XLA Modules:
  0.0 134.8 jit_solution(10742654281356507274)
XLA Ops:
  0.7 1.3 copy.11
  2.0 13.9 %while.44 = (s32[]{:T(128)}, f32[1024,128]{1,0:T(8,128)S(1)}, s32[4,4,128]{2,1,0:T(4,128)}, bf16[4,4,128,128]{2,3,1,0:T(8,128)(2,1)S(1)}, s32[4,4]{1,0:T(4,128)S...) while((s32[]{:T(128)}, f32[1024,128]{1,0:T(8,128)S(1)}, ...), condition=%wide.region_5.6_spmd.clone, body=%wide.region_4.5_spmd.clone.sunk | while | flops 287047680 | bytes 3155591 | solution.py:131
  2.7 1.2 fusion.108
  3.9 0.7 dynamic-slice_bitcast_fusion.15
  6.2 1.2 fusion.108
  7.3 0.7 dynamic-slice_bitcast_fusion.15
  9.6 1.2 fusion.108
  10.8 0.7 dynamic-slice_bitcast_fusion.15
  13.1 1.2 fusion.108
  14.3 0.7 dynamic-slice_bitcast_fusion.15
  17.5 29.2 %while.45 = (s32[]{:T(128)}, f32[2048,128]{1,0:T(8,128)S(1)}, s32[2,512,8]{1,2,0:T(8,128)S(1)}, f32[2,512,8]{1,2,0:T(8,128)S(1)}, f32[2,512,128]{2,1,0:T(8,128)S(1)}, /*index=5*/s32[]{:T(128)}, s32[]{:T(128)}) while((s32[]{:T(128)}, f32[2048,128]{1,0:T(8,128)S(1)}, s32[2,512,8]{1,2,0:T(8,128)S(1)}, f32[2,512,8]{1,2,0:T(8,128)S(1)}, ...), condition=%wide.region_7.8_spmd.clone, body=%wide.region_6.7_spmd.clone.sunk | while | flops 885194752 | bytes 7176299 | solution.py:155
  17.8 4.7 %convolution_add_fusion.7 = f32[2048,128]{1,0:T(8,128)S(1)} fusion(f32[2048,128]{1,0:T(8,128)S(1)} %get-tuple-element.560, pred[]{:T(512)S(6)} %compare.7, f32[512]{0:T(512)S(1)} %bitcast.232, s32[512]{0:T(512)S(1)} %bitcast.256, f32[512]{0:T(512)S(1)} %bitcast.235, s32[512]{0:T(512)S(1)} %bitcast.259, f32[512]{0:T(512)S(1)} %bitcast.238, ...), kind=kOutput, calls=%fused_computation.69.clone.1 | convolution fusion | flops 294125568 | bytes 2260997 | tf_op jit(solution)/shard_map/while/body/eval_jaxpr/dot_general | solution.py:38
  22.5 4.8 %convolution_add_fusion.8 = f32[2048,128]{1,0:T(8,128)S(1)} fusion(f32[2048,128]{1,0:T(8,128)S(1)} %convolution_add_fusion.7, f32[2,512,128]{2,1,0:T(8,128)S(1)} %get-tuple-element.570, s32[]{:T(128)} %get-tuple-element.559, f32[512]{0:T(512)S(1)} %bitcast.233, s32[512]{0:T(512)S(1)} %bitcast.257, f32[512]{0:T(512)S(1)} %bitcast.236, ...), kind=kOutput, calls=%fused_computation.68.clone.1 | convolution fusion | flops 294060032 | bytes 2523140 | tf_op jit(solution)/shard_map/while/body/eval_jaxpr/dot_general | solution.py:38
  27.3 4.8 %convolution_add_fusion.9 = f32[2048,128]{1,0:T(8,128)S(1)} fusion(f32[2048,128]{1,0:T(8,128)S(1)} %convolution_add_fusion.8, f32[512]{0:T(512)S(1)} %bitcast.234, s32[512]{0:T(512)S(1)} %bitcast.258, f32[512]{0:T(512)S(1)} %bitcast.237, s32[512]{0:T(512)S(1)} %bitcast.261, f32[512]{0:T(512)S(1)} %bitcast.240, s32[512]{0:T(512)S(1)} %bitcast.264, ...), kind=kOutput, calls=%fused_computation.67.clone.1 | convolution fusion | flops 297009152 | bytes 2260996 | tf_op jit(solution)/shard_map/while/body/eval_jaxpr/dot_general | solution.py:38
  32.2 4.7 %convolution_add_fusion.7 = f32[2048,128]{1,0:T(8,128)S(1)} fusion(f32[2048,128]{1,0:T(8,128)S(1)} %get-tuple-element.560, pred[]{:T(512)S(6)} %compare.7, f32[512]{0:T(512)S(1)} %bitcast.232, s32[512]{0:T(512)S(1)} %bitcast.256, f32[512]{0:T(512)S(1)} %bitcast.235, s32[512]{0:T(512)S(1)} %bitcast.259, f32[512]{0:T(512)S(1)} %bitcast.238, ...), kind=kOutput, calls=%fused_computation.69.clone.1 | convolution fusion | flops 294125568 | bytes 2260997 | tf_op jit(solution)/shard_map/while/body/eval_jaxpr/dot_general | solution.py:38
  36.9 4.8 %convolution_add_fusion.8 = f32[2048,128]{1,0:T(8,128)S(1)} fusion(f32[2048,128]{1,0:T(8,128)S(1)} %convolution_add_fusion.7, f32[2,512,128]{2,1,0:T(8,128)S(1)} %get-tuple-element.570, s32[]{:T(128)} %get-tuple-element.559, f32[512]{0:T(512)S(1)} %bitcast.233, s32[512]{0:T(512)S(1)} %bitcast.257, f32[512]{0:T(512)S(1)} %bitcast.236, ...), kind=kOutput, calls=%fused_computation.68.clone.1 | convolution fusion | flops 294060032 | bytes 2523140 | tf_op jit(solution)/shard_map/while/body/eval_jaxpr/dot_general | solution.py:38
  41.7 4.8 %convolution_add_fusion.9 = f32[2048,128]{1,0:T(8,128)S(1)} fusion(f32[2048,128]{1,0:T(8,128)S(1)} %convolution_add_fusion.8, f32[512]{0:T(512)S(1)} %bitcast.234, s32[512]{0:T(512)S(1)} %bitcast.258, f32[512]{0:T(512)S(1)} %bitcast.237, s32[512]{0:T(512)S(1)} %bitcast.261, f32[512]{0:T(512)S(1)} %bitcast.240, s32[512]{0:T(512)S(1)} %bitcast.264, ...), kind=kOutput, calls=%fused_computation.67.clone.1 | convolution fusion | flops 297009152 | bytes 2260996 | tf_op jit(solution)/shard_map/while/body/eval_jaxpr/dot_general | solution.py:38
  46.9 6.6 %collective-permute-start.4 = (bf16[256,128]{1,0:T(8,128)(2,1)S(1)}, bf16[256,128]{1,0:T(8,128)(2,1)S(1)}, u32[]{:S(2)}, u32[]{:S(2)}) collective-permute-start(bf16[256,128]{1,0:T(8,128)(2,1)S(1)} %get-tuple-element.263), channel_id=1, source_target_pairs={{0,496},{16,0},{32,16},{48,32},{64,48},{80,64},{96,80},{112,96},{1... | collective-permute-start | bytes 196616 | tf_op jit(solution)/shard_map/ppermute | solution.py:12
  53.5 1.9 %collective-permute-start.5 = (bf16[256,128]{1,0:T(8,128)(2,1)S(1)}, bf16[256,128]{1,0:T(8,128)(2,1)S(1)}, u32[]{:S(2)}, u32[]{:S(2)}) collective-permute-start(bf16[256,128]{1,0:T(8,128)(2,1)S(1)} %get-tuple-element.266), channel_id=1, source_target_pairs={{0,16},{16,32},{32,48},{48,64},{64,80},{80,96},{96,112},{112,128},... | collective-permute-start | bytes 196616 | tf_op jit(solution)/shard_map/ppermute | solution.py:12
  55.4 2.0 %collective-permute-start.6 = (bf16[256,128]{1,0:T(8,128)(2,1)S(1)}, bf16[256,128]{1,0:T(8,128)(2,1)S(1)}, u32[]{:S(2)}, u32[]{:S(2)}) collective-permute-start(bf16[256,128]{1,0:T(8,128)(2,1)S(1)} %get-tuple-element.265), channel_id=1, source_target_pairs={{1,0},{2,1},{3,2},{4,3},{5,4},{6,5},{7,6},{8,7},{9,8},{10,9},{11,1... | collective-permute-start | bytes 196616 | tf_op jit(solution)/shard_map/ppermute | solution.py:18
  57.4 5.1 %collective-permute-start.7 = (bf16[256,128]{1,0:T(8,128)(2,1)S(1)}, bf16[256,128]{1,0:T(8,128)(2,1)}, u32[]{:S(2)}, u32[]{:S(2)}) collective-permute-start(bf16[256,128]{1,0:T(8,128)(2,1)S(1)} %get-tuple-element.264), channel_id=1, source_target_pairs={{0,1},{1,2},{2,3},{3,4},{4,5},{5,6},{6,7},{7,8},{8,9},{9,10},{10,1... | collective-permute-start | bytes 196616 | tf_op jit(solution)/shard_map/ppermute | solution.py:18
  62.5 0.8 fusion.51
  63.4 1.9 %collective-permute-start = (bf16[256,128]{1,0:T(8,128)(2,1)S(1)}, bf16[256,128]{1,0:T(8,128)(2,1)S(1)}, u32[]{:S(2)}, u32[]{:S(2)}) collective-permute-start(bf16[256,128]{1,0:T(8,128)(2,1)S(1)} %get-tuple-element.270), channel_id=1, source_target_pairs={{0,16},{16,32},{32,48},{48,64},{64,80},{80,96},{96,112},{112,128},... | collective-permute-start | bytes 196616 | tf_op jit(solution)/shard_map/ppermute | solution.py:12
  66.0 6.3 %collective-permute-done = bf16[256,128]{1,0:T(8,128)(2,1)S(1)} collective-permute-done((bf16[256,128]{1,0:T(8,128)(2,1)S(1)}, bf16[256,128]{1,0:T(8,128)(2,1)S(1)}, u32[]{:S(2)}, u32[]{:S(2)}) %collective-permute-start) | collective-permute-done | bytes 65568 | tf_op jit(solution)/shard_map/ppermute | solution.py:12
  72.3 1.9 %collective-permute-start.1 = (bf16[256,128]{1,0:T(8,128)(2,1)S(1)}, bf16[256,128]{1,0:T(8,128)(2,1)S(1)}, u32[]{:S(2)}, u32[]{:S(2)}) collective-permute-start(bf16[256,128]{1,0:T(8,128)(2,1)S(1)} %get-tuple-element.269), channel_id=1, source_target_pairs={{0,496},{16,0},{32,16},{48,32},{64,48},{80,64},{96,80},{112,96},{1... | collective-permute-start | bytes 196616 | tf_op jit(solution)/shard_map/ppermute | solution.py:12
  74.2 1.9 %collective-permute-done.1 = bf16[256,128]{1,0:T(8,128)(2,1)S(1)} collective-permute-done((bf16[256,128]{1,0:T(8,128)(2,1)S(1)}, bf16[256,128]{1,0:T(8,128)(2,1)S(1)}, u32[]{:S(2)}, u32[]{:S(2)}) %collective-permute-start.1) | collective-permute-done | bytes 65568 | tf_op jit(solution)/shard_map/ppermute | solution.py:12
  76.1 3.8 %collective-permute-start.2 = (bf16[256,128]{1,0:T(8,128)(2,1)S(1)}, bf16[256,128]{1,0:T(8,128)(2,1)S(1)}, u32[]{:S(2)}, u32[]{:S(2)}) collective-permute-start(bf16[256,128]{1,0:T(8,128)(2,1)S(1)} %get-tuple-element.268), channel_id=1, source_target_pairs={{0,1},{1,2},{2,3},{3,4},{4,5},{5,6},{6,7},{7,8},{8,9},{9,10},{10,1... | collective-permute-start | bytes 196616 | tf_op jit(solution)/shard_map/ppermute | solution.py:18
  79.9 2.4 %collective-permute-done.2 = bf16[256,128]{1,0:T(8,128)(2,1)S(1)} collective-permute-done((bf16[256,128]{1,0:T(8,128)(2,1)S(1)}, bf16[256,128]{1,0:T(8,128)(2,1)S(1)}, u32[]{:S(2)}, u32[]{:S(2)}) %collective-permute-start.2) | collective-permute-done | bytes 65568 | tf_op jit(solution)/shard_map/ppermute | solution.py:18
  82.2 1.9 %collective-permute-start.3 = (bf16[256,128]{1,0:T(8,128)(2,1)S(1)}, bf16[256,128]{1,0:T(8,128)(2,1)S(1)}, u32[]{:S(2)}, u32[]{:S(2)}) collective-permute-start(bf16[256,128]{1,0:T(8,128)(2,1)S(1)} %get-tuple-element.267), channel_id=1, source_target_pairs={{1,0},{2,1},{3,2},{4,3},{5,4},{6,5},{7,6},{8,7},{9,8},{10,9},{11,1... | collective-permute-start | bytes 196616 | tf_op jit(solution)/shard_map/ppermute | solution.py:18
  84.2 5.4 %collective-permute-done.3 = bf16[256,128]{1,0:T(8,128)(2,1)S(1)} collective-permute-done((bf16[256,128]{1,0:T(8,128)(2,1)S(1)}, bf16[256,128]{1,0:T(8,128)(2,1)S(1)}, u32[]{:S(2)}, u32[]{:S(2)}) %collective-permute-start.3) | collective-permute-done | bytes 65568 | tf_op jit(solution)/shard_map/ppermute | solution.py:18
  89.6 24.5 %while.42 = (s32[]{:T(128)}, f32[2,512,128]{2,1,0:T(8,128)S(1)}, s32[2,512,8]{1,2,0:T(8,128)S(1)}, f32[2,512,8]{1,2,0:T(8,128)S(1)}, bf16[2048,128]{1,0:T(8,128)(2,1)S(1)}, /*index=5*/s32[]{:T(128)}) while((s32[]{:T(128)}, f32[2,512,128]{2,1,0:T(8,128)S(1)}, s32[2,512,8]{1,2,0:T(8,128)S(1)}, f32[2,512,8]{1,2,0:T(8,128)S(1)}, ...), condition=%wide.region_1.2_spmd, body=%wide.region_0.1_spmd.sunk | while | flops 590413824 | bytes 2031697 | solution.py:75
  89.7 6.1 %fusion.101 = f32[512,128]{1,0:T(8,128)S(1)} fusion(bf16[2048,128]{1,0:T(8,128)(2,1)S(1)} %get-tuple-element.499, f32[512]{0:T(512)S(1)} %bitcast.279, s32[512]{0:T(512)S(1)} %bitcast.295, f32[512]{0:T(512)S(1)} %bitcast.281, s32[512]{0:T(512)S(1)} %bitcast.297, f32[512]{0:T(512)S(1)} %bitcast.283, s32[512]{0:T(512)S(1)} %bitcast.299, ...), kind=kOutput, calls=%fused_computation.10.clone.1 | convolution fusion | flops 296747008 | bytes 819200 | tf_op jit(solution)/shard_map/while/body/eval_jaxpr/dot_general | solution.py:71
  95.8 6.0 %fusion.102 = f32[2,512,128]{2,1,0:T(8,128)S(1)} fusion(f32[2,512,128]{2,1,0:T(8,128)S(1)} %get-tuple-element.490, s32[]{:T(128)} %get-tuple-element.489, f32[512,128]{1,0:T(8,128)S(1)} %fusion.101, bf16[2048,128]{1,0:T(8,128)(2,1)S(1)} %get-tuple-element.499, f32[512]{0:T(512)S(1)} %bitcast.280, s32[512]{0:T(512)S(1)} %bitcast.296, ...), kind=kOutput, calls=%fused_computation.14.clone.1 | convolution fusion | flops 293666816 | bytes 1081348 | tf_op jit(solution)/shard_map/while/body/eval_jaxpr/dot_general | solution.py:71
  101.9 6.1 %fusion.101 = f32[512,128]{1,0:T(8,128)S(1)} fusion(bf16[2048,128]{1,0:T(8,128)(2,1)S(1)} %get-tuple-element.499, f32[512]{0:T(512)S(1)} %bitcast.279, s32[512]{0:T(512)S(1)} %bitcast.295, f32[512]{0:T(512)S(1)} %bitcast.281, s32[512]{0:T(512)S(1)} %bitcast.297, f32[512]{0:T(512)S(1)} %bitcast.283, s32[512]{0:T(512)S(1)} %bitcast.299, ...), kind=kOutput, calls=%fused_computation.10.clone.1 | convolution fusion | flops 296747008 | bytes 819200 | tf_op jit(solution)/shard_map/while/body/eval_jaxpr/dot_general | solution.py:71
  108.0 6.0 %fusion.102 = f32[2,512,128]{2,1,0:T(8,128)S(1)} fusion(f32[2,512,128]{2,1,0:T(8,128)S(1)} %get-tuple-element.490, s32[]{:T(128)} %get-tuple-element.489, f32[512,128]{1,0:T(8,128)S(1)} %fusion.101, bf16[2048,128]{1,0:T(8,128)(2,1)S(1)} %get-tuple-element.499, f32[512]{0:T(512)S(1)} %bitcast.280, s32[512]{0:T(512)S(1)} %bitcast.296, ...), kind=kOutput, calls=%fused_computation.14.clone.1 | convolution fusion | flops 293666816 | bytes 1081348 | tf_op jit(solution)/shard_map/while/body/eval_jaxpr/dot_general | solution.py:71
  114.6 17.1 %while.43 = (s32[]{:T(128)}, bf16[4,4,128,128]{3,2,1,0:T(8,128)(2,1)}, s32[4,4]{1,0:T(4,128)}, s32[]{:T(128)}, bf16[4,4,128,128]{3,2,1,0:T(8,128)(2,1)}, /*index...) while((s32[]{:T(128)}, bf16[4,4,128,128]{3,2,1,0:T(8,128)(2,1)}, s32[4,4]{1,0:T(4,128)}, ...), condition=%wide.region_3.4_spmd, body=%wide.region_2.3_spmd.sunk | while | flops 151715840 | bytes 531577 | solution.py:99
  114.7 1.3 compare_bitcast_fusion.4
  116.0 0.7 dynamic-slice_bitcast_fusion.14
  116.7 2.2 %fusion.105 = bf16[4,4,128,128]{3,2,1,0:T(8,128)(2,1)} fusion(bf16[4,4,128,128]{3,2,1,0:T(8,128)(2,1)} %get-tuple-element.510, s32[]{:T(128)} %get-tuple-element.509, s32[4,128]{1,0:T(4,128)S(1)} %dynamic-slice_bitcast_fusion.14, bf16[1024,128]{1,0:T(8,128)(2,1)S(1)} %get-tuple-element.523, bf16[4,4,128,128]{3,2,1,0:T(8,128)(2,1)} %get-tuple-element.521, ...), kind=kOutput, calls=%fused_computation.24.clone.1 | convolution fusion | flops 151715840 | bytes 527364 | tf_op jit(solution)/shard_map/while/body/eval_jaxpr/jrs,jsf->jrf/dot_general | solution.py:93
  118.9 1.3 compare_bitcast_fusion.4
  120.3 0.7 dynamic-slice_bitcast_fusion.14
  121.0 2.2 %fusion.105 = bf16[4,4,128,128]{3,2,1,0:T(8,128)(2,1)} fusion(bf16[4,4,128,128]{3,2,1,0:T(8,128)(2,1)} %get-tuple-element.510, s32[]{:T(128)} %get-tuple-element.509, s32[4,128]{1,0:T(4,128)S(1)} %dynamic-slice_bitcast_fusion.14, bf16[1024,128]{1,0:T(8,128)(2,1)S(1)} %get-tuple-element.523, bf16[4,4,128,128]{3,2,1,0:T(8,128)(2,1)} %get-tuple-element.521, ...), kind=kOutput, calls=%fused_computation.24.clone.1 | convolution fusion | flops 151715840 | bytes 527364 | tf_op jit(solution)/shard_map/while/body/eval_jaxpr/jrs,jsf->jrf/dot_general | solution.py:93
  123.2 1.3 compare_bitcast_fusion.4
  124.5 0.7 dynamic-slice_bitcast_fusion.14
  125.2 2.2 %fusion.105 = bf16[4,4,128,128]{3,2,1,0:T(8,128)(2,1)} fusion(bf16[4,4,128,128]{3,2,1,0:T(8,128)(2,1)} %get-tuple-element.510, s32[]{:T(128)} %get-tuple-element.509, s32[4,128]{1,0:T(4,128)S(1)} %dynamic-slice_bitcast_fusion.14, bf16[1024,128]{1,0:T(8,128)(2,1)S(1)} %get-tuple-element.523, bf16[4,4,128,128]{3,2,1,0:T(8,128)(2,1)} %get-tuple-element.521, ...), kind=kOutput, calls=%fused_computation.24.clone.1 | convolution fusion | flops 151715840 | bytes 527364 | tf_op jit(solution)/shard_map/while/body/eval_jaxpr/jrs,jsf->jrf/dot_general | solution.py:93
  127.5 1.3 compare_bitcast_fusion.4
  129.5 2.2 %fusion.105 = bf16[4,4,128,128]{3,2,1,0:T(8,128)(2,1)} fusion(bf16[4,4,128,128]{3,2,1,0:T(8,128)(2,1)} %get-tuple-element.510, s32[]{:T(128)} %get-tuple-element.509, s32[4,128]{1,0:T(4,128)S(1)} %dynamic-slice_bitcast_fusion.14, bf16[1024,128]{1,0:T(8,128)(2,1)S(1)} %get-tuple-element.523, bf16[4,4,128,128]{3,2,1,0:T(8,128)(2,1)} %get-tuple-element.521, ...), kind=kOutput, calls=%fused_computation.24.clone.1 | convolution fusion | flops 151715840 | bytes 527364 | tf_op jit(solution)/shard_map/while/body/eval_jaxpr/jrs,jsf->jrf/dot_general | solution.py:93
  131.8 3.0 %fusion.52 = bf16[1,1,1024,128]{3,2,1,0:T(8,128)(2,1)} fusion(s32[1024]{0:T(1024)S(1)} %bitcast.312, f32[2048,128]{1,0:T(8,128)S(1)} %get-tuple-element.133, bf16[256,128]{1,0:T(8,128)(2,1)} %collective-permute-done.7, bf16[256,128]{1,0:T(8,128)(2,1)S(1)} %collective-permute-done.6, bf16[256,128]{1,0:T(8,128)(2,1)S(1)} %collective-permute-done.5, ...), kind=kOutput, calls=%fused_computation.87 | convolution fusion | flops 270794752 | bytes 1052672 | tf_op jit(solution)/shard_map/dot_general | solution.py:38
  (67 shorter events, 10.2 us)
Async XLA Ops:
  2.0 14.0 %copy-start.4 = (f32[2,16,16]{2,1,0:T(8,128)S(1)}, f32[2,16,16]{2,1,0:T(8,128)}, u32[]{:S(2)}) copy-start(f32[2,16,16]{2,1,0:T(8,128)} %param.22) | copy-start | bytes 6148
  15.9 1.0 copy-start.3
  16.0 1.5 %copy-start = (s32[1,1,1024,8]{2,3,1,0:T(8,128)S(1)}, s32[1,1,1024,8]{2,3,1,0:T(8,128)}, u32[]{:S(2)}) copy-start(s32[1,1,1024,8]{2,3,1,0:T(8,128)} %param.20) | copy-start | bytes 98308
  16.0 1.5 %copy-start.1 = (f32[1,1,1024,8]{2,3,1,0:T(8,128)S(1)}, f32[1,1,1024,8]{2,3,1,0:T(8,128)}, u32[]{:S(2)}) copy-start(f32[1,1,1024,8]{2,3,1,0:T(8,128)} %param.21) | copy-start | bytes 98308
  46.8 15.7 %copy-start.5 = (s32[1,1,4,256]{3,2,1,0:T(4,128)S(1)}, s32[1,1,4,256]{3,2,1,0:T(4,128)}, u32[]{:S(2)}) copy-start(s32[1,1,4,256]{3,2,1,0:T(4,128)} %param.19) | copy-start | bytes 12292
  46.8 15.7 %copy-start.2 = (bf16[1,1,1024,128]{3,2,1,0:T(8,128)(2,1)S(1)}, bf16[1,1,1024,128]{3,2,1,0:T(8,128)(2,1)}, u32[]{:S(2)}) copy-start(bf16[1,1,1024,128]{3,2,1,0:T(8,128)(2,1)} %param.17) | copy-start | bytes 786436
  46.9 84.9 %collective-permute-start.4 = (bf16[256,128]{1,0:T(8,128)(2,1)S(1)}, bf16[256,128]{1,0:T(8,128)(2,1)S(1)}, u32[]{:S(2)}, u32[]{:S(2)}) collective-permute-start(bf16[256,128]{1,0:T(8,128)(2,1)S(1)} %get-tuple-element.263), channel_id=1, source_target_pairs={{0,496},{16,0},{32,16},{48,32},{64,48},{80,64},{96,80},{112,96},{1... | collective-permute-start | bytes 196616 | tf_op jit(solution)/shard_map/ppermute | solution.py:12
  53.5 78.3 %collective-permute-start.5 = (bf16[256,128]{1,0:T(8,128)(2,1)S(1)}, bf16[256,128]{1,0:T(8,128)(2,1)S(1)}, u32[]{:S(2)}, u32[]{:S(2)}) collective-permute-start(bf16[256,128]{1,0:T(8,128)(2,1)S(1)} %get-tuple-element.266), channel_id=1, source_target_pairs={{0,16},{16,32},{32,48},{48,64},{64,80},{80,96},{96,112},{112,128},... | collective-permute-start | bytes 196616 | tf_op jit(solution)/shard_map/ppermute | solution.py:12
  55.4 76.3 %collective-permute-start.6 = (bf16[256,128]{1,0:T(8,128)(2,1)S(1)}, bf16[256,128]{1,0:T(8,128)(2,1)S(1)}, u32[]{:S(2)}, u32[]{:S(2)}) collective-permute-start(bf16[256,128]{1,0:T(8,128)(2,1)S(1)} %get-tuple-element.265), channel_id=1, source_target_pairs={{1,0},{2,1},{3,2},{4,3},{5,4},{6,5},{7,6},{8,7},{9,8},{10,9},{11,1... | collective-permute-start | bytes 196616 | tf_op jit(solution)/shard_map/ppermute | solution.py:18
  57.4 74.4 %collective-permute-start.7 = (bf16[256,128]{1,0:T(8,128)(2,1)S(1)}, bf16[256,128]{1,0:T(8,128)(2,1)}, u32[]{:S(2)}, u32[]{:S(2)}) collective-permute-start(bf16[256,128]{1,0:T(8,128)(2,1)S(1)} %get-tuple-element.264), channel_id=1, source_target_pairs={{0,1},{1,2},{2,3},{3,4},{4,5},{5,6},{6,7},{7,8},{8,9},{9,10},{10,1... | collective-permute-start | bytes 196616 | tf_op jit(solution)/shard_map/ppermute | solution.py:18
  63.4 8.9 %collective-permute-start = (bf16[256,128]{1,0:T(8,128)(2,1)S(1)}, bf16[256,128]{1,0:T(8,128)(2,1)S(1)}, u32[]{:S(2)}, u32[]{:S(2)}) collective-permute-start(bf16[256,128]{1,0:T(8,128)(2,1)S(1)} %get-tuple-element.270), channel_id=1, source_target_pairs={{0,16},{16,32},{32,48},{48,64},{64,80},{80,96},{96,112},{112,128},... | collective-permute-start | bytes 196616 | tf_op jit(solution)/shard_map/ppermute | solution.py:12
  72.3 3.8 %collective-permute-start.1 = (bf16[256,128]{1,0:T(8,128)(2,1)S(1)}, bf16[256,128]{1,0:T(8,128)(2,1)S(1)}, u32[]{:S(2)}, u32[]{:S(2)}) collective-permute-start(bf16[256,128]{1,0:T(8,128)(2,1)S(1)} %get-tuple-element.269), channel_id=1, source_target_pairs={{0,496},{16,0},{32,16},{48,32},{64,48},{80,64},{96,80},{112,96},{1... | collective-permute-start | bytes 196616 | tf_op jit(solution)/shard_map/ppermute | solution.py:12
  76.1 6.1 %collective-permute-start.2 = (bf16[256,128]{1,0:T(8,128)(2,1)S(1)}, bf16[256,128]{1,0:T(8,128)(2,1)S(1)}, u32[]{:S(2)}, u32[]{:S(2)}) collective-permute-start(bf16[256,128]{1,0:T(8,128)(2,1)S(1)} %get-tuple-element.268), channel_id=1, source_target_pairs={{0,1},{1,2},{2,3},{3,4},{4,5},{5,6},{6,7},{7,8},{8,9},{9,10},{10,1... | collective-permute-start | bytes 196616 | tf_op jit(solution)/shard_map/ppermute | solution.py:18
  82.2 7.4 %collective-permute-start.3 = (bf16[256,128]{1,0:T(8,128)(2,1)S(1)}, bf16[256,128]{1,0:T(8,128)(2,1)S(1)}, u32[]{:S(2)}, u32[]{:S(2)}) collective-permute-start(bf16[256,128]{1,0:T(8,128)(2,1)S(1)} %get-tuple-element.267), channel_id=1, source_target_pairs={{1,0},{2,1},{3,2},{4,3},{5,4},{6,5},{7,6},{8,7},{9,8},{10,9},{11,1... | collective-permute-start | bytes 196616 | tf_op jit(solution)/shard_map/ppermute | solution.py:18
where the time goes:
time: 136 us; the launch traced here: 135 us
  matrix products  75.2 us (55%)
  starting transfers between devices  25.1 us (18%)
  waiting for transfers between devices  16 us (12%)
  local copies, waits for them, and re-layouts  8.45 us (6%)
  other arithmetic  8.33 us (6%)
    dot_general x7, matrix products, lead_dot(): lax.dot_general(left, right, (((0,), (0,)), ((), ())), preferred_element_...  31.6 us
    ppermute x4, starting transfers between devices, shifted(): lax.ppermute(value, axis, [(source, source + steps) for source in range(f...  12.7 us
    ppermute x4, starting transfers between devices, from_behind(): return lax.ppermute(value, axis, pairs)  12.4 us
    dot_general x2, matrix products, convolve(): jnp.dot(low, extended, preferred_element_type=jnp.float32)  12.2 us
    dot_general x2, matrix products, convolve(): jnp.dot(high, extended, preferred_element_type=jnp.float32)  12 us
    dot_general x4, matrix products, place_group(): jnp.einsum('jrs,jsf->jrf', weight_group, source, preferred_element_type=j...  8.99 us
    ppermute x4, waiting for transfers between devices, from_behind(): return lax.ppermute(value, axis, pairs)  8.16 us
    ppermute x4, waiting for transfers between devices, shifted(): lax.ppermute(value, axis, [(source, source + steps) for source in range(f...  7.79 us
  transfers between devices with their start and end apart: 8, of which 4 were waited for; matrix products, arithmetic and copies ran while one was open for 32% of the time, Pallas kernels for 0%

commit v1 on v0

v1 whole, which is shorter than its diff:
```python
import jax
import jax.numpy as jnp
from jax import lax
from jax.experimental import pallas as pl
from jax.experimental.pallas import tpu as pltpu
from jax.sharding import PartitionSpec as P

MEMBERS = 4
LANES = 128
GROUP = 16
BF16 = jnp.bfloat16
F32 = jnp.float32
I32 = jnp.int32
VMEM_LIMIT = 56 * 1024 * 1024


def iota(shape, dim):
    return lax.broadcasted_iota(I32, shape, dim)


def dot(left, right, left_dim=1, right_dim=0):
    return lax.dot_general(
        left, right, (((left_dim,), (right_dim,)), ((), ())), preferred_element_type=F32
    )


def neighbor_order():
    blk_odd = lax.rem(lax.axis_index("blk"), 2)
    tile_odd = lax.rem(lax.axis_index("tile"), 2)
    return (blk_odd, 1 - blk_odd, 2 + tile_odd, 3 - tile_odd)


def mixing_matrix(vert_ref):
    rows, levels = vert_ref.shape
    tall = jnp.concatenate([vert_ref[...].astype(BF16)] * MEMBERS, axis=0)
    feat = tall.shape[0]
    repeat = jnp.where(
        lax.rem(iota((levels, feat), 1), levels) == iota((levels, feat), 0), 1.0, 0.0
    ).astype(BF16)
    wide = dot(tall, repeat)
    same = lax.div(iota((feat, feat), 0), levels) == lax.div(iota((feat, feat), 1), levels)
    return jnp.where(same, wide, 0.0)


def regroup(values):
    sub = iota(values.shape, 0)
    block = lax.div(iota(values.shape, 1), GROUP)
    for bit in (1, 2, 4):
        moved = pltpu.roll(values, LANES - GROUP * bit, 1)
        values = jnp.where((sub & bit) != 0, moved, values)
    for bit in (1, 2, 4):
        moved = pltpu.roll(values, bit, 0)
        values = jnp.where((block & bit) != 0, moved, values)
    return values


def build_stencil(nb_ref, cf_ref, code_ref, low_ref, coeff_ref, s_ref):
    points = nb_ref.shape[1]
    width = s_ref.shape[1]
    low_count = LANES
    high_count = width // low_count
    lane = iota((8, LANES), 1)
    for m in range(points // LANES):
        part = slice(m * LANES, (m + 1) * LANES)
        rows = slice(m * 8, (m + 1) * 8)
        index = regroup(nb_ref[:, part])
        code_ref[rows, :] = lax.div(index, low_count) * GROUP + (lane & (GROUP - 1))
        low_ref[rows, :] = index & (low_count - 1)
        coeff_ref[rows, :] = regroup(cf_ref[:, part])
    high_rows = iota((high_count * GROUP, LANES), 0)
    low_rows = iota((low_count, LANES), 0)
    unroll = 4

    def body(step, carry):
        for u in range(unroll):
            g = step * unroll + u
            high = jnp.where(high_rows == code_ref[pl.ds(g, 1), :], 1.0, 0.0).astype(BF16)
            low = jnp.where(low_rows == low_ref[pl.ds(g, 1), :], coeff_ref[pl.ds(g, 1), :], 0.0)
            out = dot(high, low.astype(BF16), 1, 1).astype(BF16)
            start = pl.multiple_of(g * GROUP, GROUP)
            for h in range(high_count):
                s_ref[pl.ds(start, GROUP), h * low_count : (h + 1) * low_count] = out[
                    h * GROUP : (h + 1) * GROUP
                ]
        return carry

    lax.fori_loop(0, points // GROUP // unroll, body, 0)


def one_hot_columns(row, height):
    return jnp.where(iota((height, LANES), 0) == row, 1.0, 0.0).astype(BF16)


def one_hot_of_rows(row, width):
    column = jnp.broadcast_to(row.astype(F32), (LANES, LANES)).T.astype(I32)
    lane = iota((LANES, LANES), 1)
    return jnp.concatenate(
        [
            jnp.where(column == lane + c * LANES, 1.0, 0.0).astype(BF16)
            for c in range(width // LANES)
        ],
        axis=1,
    )


def adjoint_kernel(
    live_ref, field_ref, send_ref, nb_ref, cf_ref, vert_ref, w_ref, map_ref, cot_ref,
    sent0, sent1, sent2, sent3, own_ref, s_ref, pt_ref,
    code_ref, low_ref, coeff_ref, bb_ref, mbt_ref, halo_ref,
):
    order = neighbor_order()
    points = field_ref.shape[0]
    half = send_ref.shape[1]
    slots, block = map_ref.shape
    live = live_ref[0, 0]
    for slot, sent in enumerate((sent0, sent1, sent2, sent3)):
        for h in range(half // LANES):
            cols = slice(h * LANES, (h + 1) * LANES)
            first = slot // 2 * 2
            row = jnp.where(
                order[slot] == first, send_ref[first : first + 1, cols], send_ref[first + 1 : first + 2, cols]
            )
            picked = dot(one_hot_of_rows(row, points), field_ref[...])
            sent[cols, :] = picked.astype(BF16)
    for j in range(slots):
        cols = slice(j * block, (j + 1) * block)
        pt_ref[:, cols] = one_hot_columns(map_ref[j : j + 1, :], points)
        result = dot(w_ref[j], cot_ref[cols, :], 0, 0)
        bb_ref[cols, :] = jnp.where(j < live, result, 0.0).astype(BF16)
    build_stencil(nb_ref, cf_ref, code_ref, low_ref, coeff_ref, s_ref)
    mixing = mixing_matrix(vert_ref).astype(BF16)
    rows_each = 256
    for c in range(points // rows_each):
        rows = slice(c * rows_each, (c + 1) * rows_each)
        back = dot(pt_ref[rows, :], bb_ref[...]).astype(BF16)
        mbt_ref[:, rows] = dot(mixing, back, 1, 1).astype(BF16)
    for c in range(s_ref.shape[1] // half):
        cols = slice(c * half, (c + 1) * half)
        part = dot(mbt_ref[...], s_ref[:, cols]).T
        if c * half < points:
            own_ref[cols, :] = part
        else:
            halo_ref[c * half - points : (c + 1) * half - points, :] = part.astype(BF16)
    for slot, sent in enumerate((sent0, sent1, sent2, sent3)):
        start = pl.multiple_of((order[slot] ^ 1) * half, half)
        sent[half:, :] = halo_ref[pl.ds(start, half), :]


def forward_kernel(
    live_ref, got0, got1, got2, got3, field_ref, send_ref, vert_ref, w_ref, own_ref, s_ref, pt_ref,
    grid_ref, grad_ref,
    ext_ref, ret_ref, conv_ref, sel_ref,
):
    order = neighbor_order()
    points = field_ref.shape[0]
    half = send_ref.shape[1]
    slots, block = w_ref.shape[0], w_ref.shape[1]
    live = live_ref[0, 0]
    ext_ref[:points, :] = field_ref[...]
    for slot, got in enumerate((got0, got1, got2, got3)):
        start = pl.multiple_of(points + (order[slot] ^ 1) * half, half)
        ext_ref[pl.ds(start, half), :] = got[:half, :]
        ret_ref[pl.ds(pl.multiple_of(order[slot] * half, half), half), :] = got[half:, :]
    mixing = mixing_matrix(vert_ref).T.astype(BF16)
    rows_each = 256
    for c in range(points // rows_each):
        rows = slice(c * rows_each, (c + 1) * rows_each)
        horizontal = dot(s_ref[rows, :], ext_ref[...]).astype(BF16)
        conv_ref[:, rows] = dot(mixing, horizontal, 1, 1).astype(BF16)
    for j in range(0, slots, 2):
        source = dot(conv_ref[...], pt_ref[:, j * block : (j + 2) * block]).astype(BF16)
        for u in range(2):
            result = dot(w_ref[j + u], source[:, u * block : (u + 1) * block], 1, 1)
            grid_ref[(j + u) * block : (j + u + 1) * block, :] = jnp.where(
                j + u < live, result, 0.0
            ).astype(BF16)
    for q in range(4):
        for h in range(half // LANES):
            cols = slice(q * half + h * LANES, q * half + (h + 1) * LANES)
            row = send_ref[q : q + 1, h * LANES : (h + 1) * LANES]
            sel_ref[:, cols] = one_hot_columns(row, points)
    for c in range(points // rows_each):
        rows = slice(c * rows_each, (c + 1) * rows_each)
        grad_ref[rows, :] = (own_ref[rows, :] + dot(sel_ref[rows, :], ret_ref[...])).astype(BF16)


def swap_pairs(count, first):
    pairs = [(i, (i + 1) % count) for i in range(first, count, 2)]
    return pairs + [(b, a) for a, b in pairs]


def exchange(value, axis, first, cycle):
    count = lax.axis_size(axis)
    pairs = swap_pairs(count, first)
    if not cycle:
        pairs = [(a, b) for a, b in pairs if abs(a - b) == 1]
    return lax.ppermute(value, axis, pairs)


def shards(field, grid_cotangent, send_rows, neighbors, stencil, vertical, interp_weights, block_map, tally):
    field = field[0, 0]
    cotangent = grid_cotangent[0, 0]
    send = send_rows[0, 0]
    nb = neighbors[0, 0].T
    cf = stencil[0, 0].T
    weights = interp_weights[0, 0]
    mapped = block_map[0, 0]
    vert = vertical.reshape(-1, vertical.shape[-1])
    points, feat = field.shape
    half = send.shape[1]
    width = points + 4 * half
    slots, block = mapped.shape
    vmem = pl.BlockSpec(memory_space=pltpu.VMEM)
    smem = pl.BlockSpec(memory_space=pltpu.SMEM)
    params = pltpu.CompilerParams(vmem_limit_bytes=VMEM_LIMIT)
    sent_shape = jax.ShapeDtypeStruct((2 * half, feat), BF16)
    sent0, sent1, sent2, sent3, own, s_mat, pt_mat = pl.pallas_call(
        adjoint_kernel,
        out_shape=(sent_shape,) * 4 + (
            jax.ShapeDtypeStruct((points, feat), F32),
            jax.ShapeDtypeStruct((points, width), BF16),
            jax.ShapeDtypeStruct((points, slots * block), BF16),
        ),
        in_specs=[smem] + [vmem] * 8,
        out_specs=(vmem,) * 7,
        scratch_shapes=[
            pltpu.VMEM((points // GROUP, LANES), I32),
            pltpu.VMEM((points // GROUP, LANES), I32),
            pltpu.VMEM((points // GROUP, LANES), F32),
            pltpu.VMEM((slots * block, feat), BF16),
            pltpu.VMEM((feat, points), BF16),
            pltpu.VMEM((4 * half, feat), BF16),
        ],
        compiler_params=params,
        cost_estimate=pl.CostEstimate(flops=10**9, bytes_accessed=8 * 10**6, transcendentals=0),
    )(tally, field, send, nb, cf, vert, weights, mapped, cotangent)
    got1 = exchange(sent1, "blk", 1, True)
    got3 = exchange(sent3, "tile", 1, False)
    got2 = exchange(sent2, "tile", 0, False)
    got0 = exchange(sent0, "blk", 0, True)
    grid, grad = pl.pallas_call(
        forward_kernel,
        out_shape=(
            jax.ShapeDtypeStruct((slots * block, feat), BF16),
            jax.ShapeDtypeStruct((points, feat), BF16),
        ),
        in_specs=[smem] + [vmem] * 11,
        out_specs=(vmem, vmem),
        scratch_shapes=[
            pltpu.VMEM((width, feat), BF16),
            pltpu.VMEM((4 * half, feat), BF16),
            pltpu.VMEM((feat, points), BF16),
            pltpu.VMEM((points, 4 * half), BF16),
        ],
        compiler_params=params,
        cost_estimate=pl.CostEstimate(flops=10**9, bytes_accessed=8 * 10**6, transcendentals=0),
    )(tally, got0, got1, got2, got3, field, send, vert, weights, own, s_mat, pt_mat)
    return grid[None, None], grad[None, None]


def solution(mesh):
    four = P("blk", "tile", None, None)
    in_specs = (four, four, four, four, four, P(), P("blk", "tile", None, None, None), four, P("blk", "tile"))
    return jax.shard_map(shards, mesh=mesh, in_specs=in_specs, out_specs=(four, four), check_vma=False)
```

time: 136 us -> 46 us (0.34)
  the two profiles are of different devices: /device:TPU:96 before, /device:TPU:128 now
where the time goes in v1:
time: 46 us; the launch traced here: 45.8 us
  Pallas kernels  22.6 us (49%)
  starting transfers between devices  14.9 us (32%)
  waiting for transfers between devices  6.32 us (14%)
  between operations  1.35 us (3%)
  local copies, waits for them, and re-layouts  0.64 us (1%)
    ppermute x4, starting transfers between devices, exchange(): return lax.ppermute(value, axis, pairs)  14.9 us
    pallas_call x1, Pallas kernels, shards(): pl.pallas_call(adjoint_kernel, out_shape=(sent_shape,) * 4 + (jax.ShapeDt...  12.5 us
    pallas_call x1, Pallas kernels, shards(): pl.pallas_call(forward_kernel, out_shape=(jax.ShapeDtypeStruct((slots * b...  10.2 us
    ppermute x4, waiting for transfers between devices, exchange(): return lax.ppermute(value, axis, pairs)  6.32 us
  transfers between devices with their start and end apart: 4, of which 2 were waited for; matrix products, arithmetic and copies ran while one was open for 0% of the time, Pallas kernels for 0%

profile of v1, /device:TPU:128, one launch (start us, length us, event | category | flops | bytes accessed | tf_op | source)
XLA Modules:
  0.0 45.8 jit_solution(4420019474347295494)
XLA Ops:
  1.3 12.5 %shard_map.104 = (bf16[512,128]{1,0:T(8,128)(2,1)}, bf16[512,128]{1,0:T(8,128)(2,1)}, bf16[512,128]{1,0:T(8,128)(2,1)}, bf16[512,128]{1,0:T(8,128)(2,1)}, f32[10...) custom-call(s32[1,1]{1,0:T(1,128)S(6)} %copy.11.live_ref, bf16[1024,128]{1,0:T(8,128)(2,1)} %bitcast.16, ...), custom_call_target="tpu_custom_call" | custom-call | flops 1000000000 | bytes 8000000 | tf_op jit(solution)/shard_map/pallas_call | solution.py:217
  13.7 1.9 %collective-permute-start = (bf16[512,128]{1,0:T(8,128)(2,1)}, bf16[512,128]{1,0:T(8,128)(2,1)S(1)}, u32[]{:S(2)}, u32[]{:S(2)}) collective-permute-start(bf16[512,128]{1,0:T(8,128)(2,1)} %get-tuple-element.11), channel_id=1, source_target_pairs={{0,16},{32,48},{64,80},{96,112},{128,144},{160,176},{192,208},{224... | collective-permute-start | bytes 393224 | tf_op jit(solution)/shard_map/ppermute | solution.py:197
  15.7 7.2 %collective-permute-start.1 = (bf16[512,128]{1,0:T(8,128)(2,1)}, bf16[512,128]{1,0:T(8,128)(2,1)S(1)}, u32[]{:S(2)}, u32[]{:S(2)}) collective-permute-start(bf16[512,128]{1,0:T(8,128)(2,1)} %get-tuple-element.12), channel_id=1, source_target_pairs={{16,32},{48,64},{80,96},{112,128},{144,160},{176,192},{208,224},{2... | collective-permute-start | bytes 393224 | tf_op jit(solution)/shard_map/ppermute | solution.py:197
  22.9 3.8 %collective-permute-start.2 = (bf16[512,128]{1,0:T(8,128)(2,1)}, bf16[512,128]{1,0:T(8,128)(2,1)S(1)}, u32[]{:S(2)}, u32[]{:S(2)}) collective-permute-start(bf16[512,128]{1,0:T(8,128)(2,1)} %get-tuple-element.13), channel_id=1, source_target_pairs={{0,1},{2,3},{4,5},{6,7},{8,9},{10,11},{12,13},{14,15},{1,0},{3,2},... | collective-permute-start | bytes 393224 | tf_op jit(solution)/shard_map/ppermute | solution.py:197
  26.7 1.9 %collective-permute-start.3 = (bf16[512,128]{1,0:T(8,128)(2,1)}, bf16[512,128]{1,0:T(8,128)(2,1)S(1)}, u32[]{:S(2)}, u32[]{:S(2)}) collective-permute-start(bf16[512,128]{1,0:T(8,128)(2,1)} %get-tuple-element.14), channel_id=1, source_target_pairs={{1,2},{3,4},{5,6},{7,8},{9,10},{11,12},{13,14},{2,1},{4,3},{6,5},{... | collective-permute-start | bytes 393224 | tf_op jit(solution)/shard_map/ppermute | solution.py:197
  28.6 0.0 collective-permute-done.got0
  28.6 0.0 copy-start
  28.7 0.0 collective-permute-done.1.got1
  28.7 0.0 copy-start.1
  28.7 1.3 %collective-permute-done.2.got2 = bf16[512,128]{1,0:T(8,128)(2,1)S(1)} collective-permute-done((bf16[512,128]{1,0:T(8,128)(2,1)}, bf16[512,128]{1,0:T(8,128)(2,1)S(1)}, u32[]{:S(2)}, u32[]{:S(2)}) %collective-permute-start.2) | collective-permute-done | bytes 131104 | tf_op jit(solution)/shard_map/ppermute | solution.py:197
  30.0 0.0 copy-start.2
  30.0 5.0 %collective-permute-done.3.got3 = bf16[512,128]{1,0:T(8,128)(2,1)S(1)} collective-permute-done((bf16[512,128]{1,0:T(8,128)(2,1)}, bf16[512,128]{1,0:T(8,128)(2,1)S(1)}, u32[]{:S(2)}, u32[]{:S(2)}) %collective-permute-start.3) | collective-permute-done | bytes 131104 | tf_op jit(solution)/shard_map/ppermute | solution.py:197
  35.0 0.0 copy-start.3
  35.0 0.0 copy-done
  35.0 0.0 copy-done.1
  35.0 0.0 copy-done.2
  35.0 0.6 %copy-done.3 = bf16[512,128]{1,0:T(8,128)(2,1)} copy-done((bf16[512,128]{1,0:T(8,128)(2,1)}, bf16[512,128]{1,0:T(8,128)(2,1)S(1)}, u32[]{:S(2)}) %copy-start.3) | copy-done | bytes 131096
  35.6 10.2 %shard_map.105 = (bf16[2048,128]{1,0:T(8,128)(2,1)}, bf16[1024,128]{1,0:T(8,128)(2,1)}) custom-call(s32[1,1]{1,0:T(1,128)S(6)} %copy.11.live_ref, bf16[512,128]{1,0:T(8,128)(2,1)} %copy-done, bf16[512,128]{1,0:T(8,128)(2,1)} %copy-done.1, bf16[512,128]{1,0:T(8,128)(2,1)} %copy-done.2, bf16[512,128]{1,0:T(8,128)(2,1)} %copy-done.3, ...), custom_call_target="tpu_custom_call" | custom-call | flops 1000000000 | bytes 8000000 | tf_op jit(solution)/shard_map/pallas_call | solution.py:241
Async XLA Ops:
  13.7 14.9 %collective-permute-start = (bf16[512,128]{1,0:T(8,128)(2,1)}, bf16[512,128]{1,0:T(8,128)(2,1)S(1)}, u32[]{:S(2)}, u32[]{:S(2)}) collective-permute-start(bf16[512,128]{1,0:T(8,128)(2,1)} %get-tuple-element.11), channel_id=1, source_target_pairs={{0,16},{32,48},{64,80},{96,112},{128,144},{160,176},{192,208},{224... | collective-permute-start | bytes 393224 | tf_op jit(solution)/shard_map/ppermute | solution.py:197
  15.7 13.0 %collective-permute-start.1 = (bf16[512,128]{1,0:T(8,128)(2,1)}, bf16[512,128]{1,0:T(8,128)(2,1)S(1)}, u32[]{:S(2)}, u32[]{:S(2)}) collective-permute-start(bf16[512,128]{1,0:T(8,128)(2,1)} %get-tuple-element.12), channel_id=1, source_target_pairs={{16,32},{48,64},{80,96},{112,128},{144,160},{176,192},{208,224},{2... | collective-permute-start | bytes 393224 | tf_op jit(solution)/shard_map/ppermute | solution.py:197
  22.9 7.1 %collective-permute-start.2 = (bf16[512,128]{1,0:T(8,128)(2,1)}, bf16[512,128]{1,0:T(8,128)(2,1)S(1)}, u32[]{:S(2)}, u32[]{:S(2)}) collective-permute-start(bf16[512,128]{1,0:T(8,128)(2,1)} %get-tuple-element.13), channel_id=1, source_target_pairs={{0,1},{2,3},{4,5},{6,7},{8,9},{10,11},{12,13},{14,15},{1,0},{3,2},... | collective-permute-start | bytes 393224 | tf_op jit(solution)/shard_map/ppermute | solution.py:197
  26.7 8.3 %collective-permute-start.3 = (bf16[512,128]{1,0:T(8,128)(2,1)}, bf16[512,128]{1,0:T(8,128)(2,1)S(1)}, u32[]{:S(2)}, u32[]{:S(2)}) collective-permute-start(bf16[512,128]{1,0:T(8,128)(2,1)} %get-tuple-element.14), channel_id=1, source_target_pairs={{1,2},{3,4},{5,6},{7,8},{9,10},{11,12},{13,14},{2,1},{4,3},{6,5},{... | collective-permute-start | bytes 393224 | tf_op jit(solution)/shard_map/ppermute | solution.py:197
  28.6 6.3 %copy-start = (bf16[512,128]{1,0:T(8,128)(2,1)}, bf16[512,128]{1,0:T(8,128)(2,1)S(1)}, u32[]{:S(2)}) copy-start(bf16[512,128]{1,0:T(8,128)(2,1)S(1)} %collective-permute-done.got0) | copy-start | bytes 393220
  28.7 6.3 %copy-start.1 = (bf16[512,128]{1,0:T(8,128)(2,1)}, bf16[512,128]{1,0:T(8,128)(2,1)S(1)}, u32[]{:S(2)}) copy-start(bf16[512,128]{1,0:T(8,128)(2,1)S(1)} %collective-permute-done.1.got1) | copy-start | bytes 393220
  30.0 5.0 %copy-start.2 = (bf16[512,128]{1,0:T(8,128)(2,1)}, bf16[512,128]{1,0:T(8,128)(2,1)S(1)}, u32[]{:S(2)}) copy-start(bf16[512,128]{1,0:T(8,128)(2,1)S(1)} %collective-permute-done.2.got2) | copy-start | bytes 393220
  35.0 0.6 %copy-start.3 = (bf16[512,128]{1,0:T(8,128)(2,1)}, bf16[512,128]{1,0:T(8,128)(2,1)S(1)}, u32[]{:S(2)}) copy-start(bf16[512,128]{1,0:T(8,128)(2,1)S(1)} %collective-permute-done.3.got3) | copy-start | bytes 393220

commit v2 on v1

v2 whole, which is shorter than its diff:
```python
import jax
import jax.numpy as jnp
from jax import lax
from jax.experimental import pallas as pl
from jax.experimental.pallas import tpu as pltpu
from jax.sharding import PartitionSpec as P

MEMBERS = 4
LANES = 128
GROUP = 16
LOW = 256
CHUNK = 256
BF16 = jnp.bfloat16
F32 = jnp.float32
I32 = jnp.int32
VMEM_LIMIT = 20 * 1024 * 1024


def iota(shape, dim):
    return lax.broadcasted_iota(I32, shape, dim)


def dot(left, right, left_dim=1, right_dim=0):
    return lax.dot_general(
        left, right, (((left_dim,), (right_dim,)), ((), ())), preferred_element_type=F32
    )


def neighbor_order():
    blk_odd = lax.rem(lax.axis_index("blk"), 2)
    tile_odd = lax.rem(lax.axis_index("tile"), 2)
    return (blk_odd, 1 - blk_odd, 2 + tile_odd, 3 - tile_odd)


def mixing_matrix(vertical):
    levels = vertical.shape[1]
    tall = jnp.concatenate([vertical.astype(BF16)] * MEMBERS, axis=0)
    feat = tall.shape[0]
    repeat = jnp.where(
        lax.rem(iota((levels, feat), 1), levels) == iota((levels, feat), 0), 1.0, 0.0
    ).astype(BF16)
    wide = dot(tall, repeat)
    same = lax.div(iota((feat, feat), 0), levels) == lax.div(iota((feat, feat), 1), levels)
    return jnp.where(same, wide, 0.0)


def regroup(values):
    sub = iota(values.shape, 0)
    block = lax.div(iota(values.shape, 1), GROUP)
    for bit in (1, 2, 4):
        moved = pltpu.roll(values, LANES - GROUP * bit, 1)
        values = jnp.where((sub & bit) != 0, moved, values)
    for bit in (1, 2, 4):
        moved = pltpu.roll(values, bit, 0)
        values = jnp.where((block & bit) != 0, moved, values)
    return values


def build_stencil(nb_ref, cf_ref, code_ref, low_ref, coeff_ref, s_ref):
    points = nb_ref.shape[1]
    high_count = s_ref.shape[1] // LOW
    lane = iota((8, LANES), 1)
    for m in range(points // LANES):
        part = slice(m * LANES, (m + 1) * LANES)
        rows = slice(m * 8, (m + 1) * 8)
        index = regroup(nb_ref[:, part])
        code_ref[rows, :] = lax.div(index, LOW) * GROUP + (lane & (GROUP - 1))
        low_ref[rows, :] = index & (LOW - 1)
        coeff_ref[rows, :] = regroup(cf_ref[:, part])
    high_rows = iota((high_count * GROUP, LANES), 0)
    low_rows = iota((LOW, LANES), 0)
    for g in range(points // GROUP):
        high = jnp.where(high_rows == code_ref[g : g + 1, :], 1.0, 0.0).astype(BF16)
        low = jnp.where(low_rows == low_ref[g : g + 1, :], coeff_ref[g : g + 1, :], 0.0)
        out = dot(high, low.astype(BF16), 1, 1).astype(BF16)
        for h in range(high_count):
            s_ref[g * GROUP : (g + 1) * GROUP, h * LOW : (h + 1) * LOW] = out[
                h * GROUP : (h + 1) * GROUP
            ]


def one_hot_columns(row, height):
    return jnp.where(iota((height, LANES), 0) == row, 1.0, 0.0).astype(BF16)


def adjoint_kernel(
    live_ref, field_hbm, send_hbm, nb_hbm, cf_hbm, vert_hbm, w_hbm, map_hbm, cot_hbm,
    sent0, sent1, sent2, sent3, s_ref, pt_ref, mbt_ref, field_ref, send_ref, w_ref, mix_ref,
    nb_ref, cf_ref, vert_ref, map_ref, cot_ref,
    code_ref, low_ref, coeff_ref, bb_ref, back_ref, sems,
):
    order = neighbor_order()
    points = field_ref.shape[0]
    half = send_ref.shape[1]
    slots, block = map_ref.shape
    live = live_ref[0, 0]
    pairs = (
        (nb_hbm, nb_ref), (cf_hbm, cf_ref), (map_hbm, map_ref), (w_hbm, w_ref), (cot_hbm, cot_ref),
        (vert_hbm, vert_ref), (send_hbm, send_ref), (field_hbm, field_ref),
    )
    copies = [pltpu.make_async_copy(a, b, sems.at[i]) for i, (a, b) in enumerate(pairs)]
    for copy in copies:
        copy.start()
    copies[0].wait()
    copies[1].wait()
    build_stencil(nb_ref, cf_ref, code_ref, low_ref, coeff_ref, s_ref)
    for copy in copies[2:]:
        copy.wait()
    for j in range(slots):
        cols = slice(j * block, (j + 1) * block)
        pt_ref[:, cols] = one_hot_columns(map_ref[j : j + 1, :], points)
        result = dot(w_ref[j], cot_ref[cols, :], 0, 0)
        bb_ref[cols, :] = jnp.where(j < live, result, 0.0).astype(BF16)
    mixing = mixing_matrix(vert_ref[...])
    mix_ref[...] = mixing.T.astype(BF16)
    for c in range(points // CHUNK):
        rows = slice(c * CHUNK, (c + 1) * CHUNK)
        back_ref[rows, :] = dot(pt_ref[rows, :], bb_ref[...]).astype(BF16)
    mbt_ref[...] = dot(mixing.astype(BF16), back_ref[...], 1, 1).astype(BF16)
    field_t = field_ref[...].T
    for slot, sent in enumerate((sent0, sent1, sent2, sent3)):
        columns = []
        for h in range(half // LANES):
            lanes = slice(h * LANES, (h + 1) * LANES)
            first = slot // 2 * 2
            row = jnp.where(
                order[slot] == first, send_ref[first : first + 1, lanes], send_ref[first + 1 : first + 2, lanes]
            )
            columns.append(one_hot_columns(row, points))
        sent[:half, :] = dot(field_t, jnp.concatenate(columns, axis=1)).T.astype(BF16)
        start = pl.multiple_of(points + (order[slot] ^ 1) * half, half)
        sent[half:, :] = dot(mbt_ref[...], s_ref[:, pl.ds(start, half)]).T.astype(BF16)


def local_kernel(mbt_ref, s_ref, field_ref, send_ref, own_ref, hor_ref, sel_ref):
    points = field_ref.shape[0]
    half = send_ref.shape[1]
    for c in range(points // CHUNK):
        rows = slice(c * CHUNK, (c + 1) * CHUNK)
        own_ref[rows, :] = dot(mbt_ref[...], s_ref[:, rows]).T
        hor_ref[rows, :] = dot(s_ref[rows, :points], field_ref[...])
    for q in range(4):
        for h in range(half // LANES):
            cols = slice(q * half + h * LANES, q * half + (h + 1) * LANES)
            row = send_ref[q : q + 1, h * LANES : (h + 1) * LANES]
            sel_ref[:, cols] = one_hot_columns(row, points)


def forward_kernel(
    live_ref, got0, got1, got2, got3, s_ref, pt_ref, w_ref, mix_ref, own_ref, hor_ref, sel_ref,
    grid_hbm, grad_hbm,
    halo_ref, ret_ref, hb_ref, conv_ref, src_ref, grid_ref, grad_ref, sems,
):
    order = neighbor_order()
    points = hor_ref.shape[0]
    half = got0.shape[0] // 2
    slots, block = w_ref.shape[0], w_ref.shape[1]
    live = live_ref[0, 0]
    for slot, got in enumerate((got0, got1, got2, got3)):
        start = pl.multiple_of((order[slot] ^ 1) * half, half)
        halo_ref[pl.ds(start, half), :] = got[:half, :]
        ret_ref[pl.ds(pl.multiple_of(order[slot] * half, half), half), :] = got[half:, :]
    for c in range(points // CHUNK):
        rows = slice(c * CHUNK, (c + 1) * CHUNK)
        hb_ref[rows, :] = (hor_ref[rows, :] + dot(s_ref[rows, points:], halo_ref[...])).astype(BF16)
    conv_ref[...] = dot(mix_ref[...], hb_ref[...], 1, 1).astype(BF16)
    for c in range(points // CHUNK):
        rows = slice(c * CHUNK, (c + 1) * CHUNK)
        grad_ref[rows, :] = (own_ref[rows, :] + dot(sel_ref[rows, :], ret_ref[...])).astype(BF16)
    copies = [pltpu.make_async_copy(grad_ref, grad_hbm, sems.at[0])]
    copies[0].start()
    for c in range(slots * block // CHUNK):
        cols = slice(c * CHUNK, (c + 1) * CHUNK)
        src_ref[cols, :] = dot(conv_ref[...], pt_ref[:, cols]).T.astype(BF16)
    quarter = slots // 4
    for j in range(slots):
        rows = slice(j * block, (j + 1) * block)
        result = dot(w_ref[j], src_ref[rows, :])
        grid_ref[rows, :] = jnp.where(j < live, result, 0.0).astype(BF16)
        if j % quarter == quarter - 1:
            part = pl.ds((j + 1 - quarter) * block, quarter * block)
            copies.append(pltpu.make_async_copy(grid_ref.at[part], grid_hbm.at[part], sems.at[len(copies)]))
            copies[-1].start()
    for copy in copies:
        copy.wait()


def exchange(value, axis, first, cycle):
    count = lax.axis_size(axis)
    pairs = [(i, (i + 1) % count) for i in range(first, count, 2)]
    if not cycle:
        pairs = [(a, b) for a, b in pairs if a < b]
    return lax.ppermute(value, axis, pairs + [(b, a) for a, b in pairs])


def shards(field, grid_cotangent, send_rows, neighbors, stencil, vertical, interp_weights, block_map, tally):
    field = field[0, 0]
    cotangent = grid_cotangent[0, 0]
    send = send_rows[0, 0]
    nb = neighbors[0, 0].T
    cf = stencil[0, 0].T
    weights = interp_weights[0, 0]
    mapped = block_map[0, 0]
    vert = vertical.reshape(-1, vertical.shape[-1])
    points, feat = field.shape
    half = send.shape[1]
    width = points + 4 * half
    slots, block = mapped.shape
    vmem = pl.BlockSpec(memory_space=pltpu.VMEM)
    smem = pl.BlockSpec(memory_space=pltpu.SMEM)
    hbm = pl.BlockSpec(memory_space=pltpu.HBM)

    def in_vmem(*values):
        return [pltpu.with_memory_space_constraint(value, pltpu.VMEM) for value in values]

    def in_hbm(*values):
        return [pltpu.with_memory_space_constraint(value, pltpu.HBM) for value in values]

    def cost(flops):
        return pl.CostEstimate(flops=flops, bytes_accessed=10**6, transcendentals=0)

    params = pltpu.CompilerParams(vmem_limit_bytes=VMEM_LIMIT)
    shared = (
        pltpu.VMEM((points, width), BF16),
        pltpu.VMEM((points, slots * block), BF16),
        pltpu.VMEM((feat, points), BF16),
        pltpu.VMEM(field.shape, BF16),
        pltpu.VMEM(send.shape, I32),
        pltpu.VMEM(weights.shape, BF16),
        pltpu.VMEM((feat, feat), BF16),
    )
    sent0, sent1, sent2, sent3, s_mat, pt_mat, mbt, field_v, send_v, w_v, mix = pl.pallas_call(
        adjoint_kernel,
        out_shape=(pltpu.VMEM((2 * half, feat), BF16),) * 4 + shared,
        in_specs=[smem] + [hbm] * 8,
        out_specs=(vmem,) * 11,
        scratch_shapes=[
            pltpu.VMEM(nb.shape, I32),
            pltpu.VMEM(cf.shape, F32),
            pltpu.VMEM(vert.shape, F32),
            pltpu.VMEM(mapped.shape, I32),
            pltpu.VMEM(cotangent.shape, BF16),
            pltpu.VMEM((points // GROUP, LANES), I32),
            pltpu.VMEM((points // GROUP, LANES), I32),
            pltpu.VMEM((points // GROUP, LANES), F32),
            pltpu.VMEM((slots * block, feat), BF16),
            pltpu.VMEM((points, feat), BF16),
            pltpu.SemaphoreType.DMA((8,)),
        ],
        compiler_params=params,
        cost_estimate=cost(2 * 10**9),
    )(tally, *in_hbm(field, send, nb, cf, vert, weights, mapped, cotangent))
    got0 = exchange(sent0, "blk", 0, True)
    got1 = exchange(sent1, "blk", 1, True)
    got2 = exchange(sent2, "tile", 0, False)
    got3 = exchange(sent3, "tile", 1, False)
    own, hor, sel = pl.pallas_call(
        local_kernel,
        out_shape=(
            pltpu.VMEM((points, feat), F32),
            pltpu.VMEM((points, feat), F32),
            pltpu.VMEM((points, 4 * half), BF16),
        ),
        in_specs=[vmem] * 4,
        out_specs=(vmem,) * 3,
        compiler_params=params,
        cost_estimate=cost(10**9),
    )(*in_vmem(mbt, s_mat, field_v, send_v))
    grid, grad = pl.pallas_call(
        forward_kernel,
        out_shape=(
            pltpu.HBM((slots * block, feat), BF16),
            pltpu.HBM((points, feat), BF16),
        ),
        in_specs=[smem] + [vmem] * 11,
        out_specs=(hbm, hbm),
        scratch_shapes=[
            pltpu.VMEM((4 * half, feat), BF16),
            pltpu.VMEM((4 * half, feat), BF16),
            pltpu.VMEM((points, feat), BF16),
            pltpu.VMEM((feat, points), BF16),
            pltpu.VMEM((slots * block, feat), BF16),
            pltpu.VMEM((slots * block, feat), BF16),
            pltpu.VMEM((points, feat), BF16),
            pltpu.SemaphoreType.DMA((5,)),
        ],
        compiler_params=params,
        cost_estimate=cost(10**9),
    )(tally, *in_vmem(got0, got1, got2, got3, s_mat, pt_mat, w_v, mix, own, hor, sel))
    return grid[None, None], grad[None, None]


def solution(mesh):
    four = P("blk", "tile", None, None)
    in_specs = (four, four, four, four, four, P(), P("blk", "tile", None, None, None), four, P("blk", "tile"))
    return jax.shard_map(shards, mesh=mesh, in_specs=in_specs, out_specs=(four, four), check_vma=False)
```

time: 46 us -> 31 us (0.67)
  Pallas kernels: 22.6 us -> 10.6 us
  waiting for transfers between devices: 6.32 us -> 3.94 us
  local copies, waits for them, and re-layouts: 0.64 us -> 0 us
    pallas_call x2 -> x3, Pallas kernels: 22.6 us -> 10.6 us  [the longest x1 5.46 us: shards(): pl.pallas_call(adjoint_kernel, out_shape=(pltpu.VMEM((2 * half, feat), BF...]
    ppermute x4, waiting for transfers between devices: 6.32 us -> 3.94 us  [exchange(): return lax.ppermute(value, axis, pairs + [(b, a) for a, b in pairs])]
    unnamed x8 -> x0, local copies, waits for them, and re-layouts: 0.64 us -> none
  transfers between devices with their start and end apart: 4 -> 4, of which waited for: 2 -> 1; matrix products, arithmetic and copies ran while one was open for 0% -> 0% of each run, Pallas kernels for 0% -> 7%
where the time goes in v2:
time: 31 us; the launch traced here: 30.8 us
  starting transfers between devices  14.9 us (48%)
  Pallas kernels  10.6 us (34%)
  waiting for transfers between devices  3.94 us (13%)
  between operations  1.35 us (4%)
    ppermute x4, starting transfers between devices, exchange(): return lax.ppermute(value, axis, pairs + [(b, a) for a, b in pairs])  14.9 us
    pallas_call x1, Pallas kernels, shards(): pl.pallas_call(adjoint_kernel, out_shape=(pltpu.VMEM((2 * half, feat), BF...  5.46 us
    ppermute x4, waiting for transfers between devices, exchange(): return lax.ppermute(value, axis, pairs + [(b, a) for a, b in pairs])  3.94 us
    pallas_call x1, Pallas kernels, shards(): pl.pallas_call(forward_kernel, out_shape=(pltpu.HBM((slots * block, feat)...  3.01 us
    pallas_call x1, Pallas kernels, shards(): pl.pallas_call(local_kernel, out_shape=(pltpu.VMEM((points, feat), F32),...  2.17 us
  transfers between devices with their start and end apart: 4, of which 1 were waited for; matrix products, arithmetic and copies ran while one was open for 0% of the time, Pallas kernels for 7%

profile of v2, /device:TPU:128, one launch (start us, length us, event | category | flops | bytes accessed | tf_op | source)
XLA Modules:
  0.0 30.8 jit_solution(3366739681407983067)
XLA Ops:
  1.3 5.5 %shard_map.104 = (bf16[512,128]{1,0:T(8,128)(2,1)S(1)}, bf16[512,128]{1,0:T(8,128)(2,1)S(1)}, bf16[512,128]{1,0:T(8,128)(2,1)S(1)}, bf16[512,128]{1,0:T(8,128)(2...) custom-call(s32[1,1]{1,0:T(1,128)S(6)} %copy.11.live_ref, ...), custom_call_target="tpu_custom_call" | custom-call | flops 2000000000 | bytes 1000000 | tf_op jit(solution)/shard_map/pallas_call | solution.py:232
  6.8 1.9 %collective-permute-start = (bf16[512,128]{1,0:T(8,128)(2,1)S(1)}, bf16[512,128]{1,0:T(8,128)(2,1)S(1)}, u32[]{:S(2)}, u32[]{:S(2)}) collective-permute-start(bf16[512,128]{1,0:T(8,128)(2,1)S(1)} %get-tuple-element.18), channel_id=1, source_target_pairs={{0,16},{32,48},{64,80},{96,112},{128,144},{160,176},{192,208},{224... | collective-permute-start | bytes 393224 | tf_op jit(solution)/shard_map/ppermute | solution.py:193
  8.7 7.2 %collective-permute-start.1 = (bf16[512,128]{1,0:T(8,128)(2,1)S(1)}, bf16[512,128]{1,0:T(8,128)(2,1)S(1)}, u32[]{:S(2)}, u32[]{:S(2)}) collective-permute-start(bf16[512,128]{1,0:T(8,128)(2,1)S(1)} %get-tuple-element.19), channel_id=1, source_target_pairs={{16,32},{48,64},{80,96},{112,128},{144,160},{176,192},{208,224},{2... | collective-permute-start | bytes 393224 | tf_op jit(solution)/shard_map/ppermute | solution.py:193
  15.9 3.8 %collective-permute-start.2 = (bf16[512,128]{1,0:T(8,128)(2,1)S(1)}, bf16[512,128]{1,0:T(8,128)(2,1)S(1)}, u32[]{:S(2)}, u32[]{:S(2)}) collective-permute-start(bf16[512,128]{1,0:T(8,128)(2,1)S(1)} %get-tuple-element.20), channel_id=1, source_target_pairs={{0,1},{2,3},{4,5},{6,7},{8,9},{10,11},{12,13},{14,15},{1,0},{3,2},... | collective-permute-start | bytes 393224 | tf_op jit(solution)/shard_map/ppermute | solution.py:193
  19.7 1.9 %collective-permute-start.3 = (bf16[512,128]{1,0:T(8,128)(2,1)S(1)}, bf16[512,128]{1,0:T(8,128)(2,1)S(1)}, u32[]{:S(2)}, u32[]{:S(2)}) collective-permute-start(bf16[512,128]{1,0:T(8,128)(2,1)S(1)} %get-tuple-element.21), channel_id=1, source_target_pairs={{1,2},{3,4},{5,6},{7,8},{9,10},{11,12},{13,14},{2,1},{4,3},{6,5},{... | collective-permute-start | bytes 393224 | tf_op jit(solution)/shard_map/ppermute | solution.py:193
  21.7 2.2 %shard_map.105 = (f32[1024,128]{1,0:T(8,128)S(1)}, f32[1024,128]{1,0:T(8,128)S(1)}, bf16[1024,1024]{1,0:T(8,128)(2,1)S(1)}) custom-call(bf16[128,1024]{1,0:T(8,128)(2,1)S(1)} %get-tuple-element.26.mbt_ref, bf16[1024,2048]{1,0:T(8,128)(2,1)S(1)} %get-tuple-element.22.s_ref, bf16[1024,128]{1,0:T(8,128)(2,1)S(1)} %get-tuple-element.27.field_ref, ...), custom_call_target="tpu_custom_call" | custom-call | flops 1000000000 | bytes 1000000 | tf_op jit(solution)/shard_map/pallas_call | solution.py:257
  23.8 0.0 collective-permute-done.got0
  23.8 0.0 collective-permute-done.1.got1
  23.9 0.0 collective-permute-done.2.got2
  23.9 3.9 %collective-permute-done.3.got3 = bf16[512,128]{1,0:T(8,128)(2,1)S(1)} collective-permute-done((bf16[512,128]{1,0:T(8,128)(2,1)S(1)}, bf16[512,128]{1,0:T(8,128)(2,1)S(1)}, u32[]{:S(2)}, u32[]{:S(2)}) %collective-permute-start.3) | collective-permute-done | bytes 131104 | tf_op jit(solution)/shard_map/ppermute | solution.py:193
  27.8 3.0 %shard_map.106 = (bf16[2048,128]{1,0:T(8,128)(2,1)}, bf16[1024,128]{1,0:T(8,128)(2,1)}) custom-call(s32[1,1]{1,0:T(1,128)S(6)} %copy.11.live_ref, bf16[512,128]{1,0:T(8,128)(2,1)S(1)} %collective-permute-done.got0, bf16[512,128]{1,0:T(8,128)(2,1)S(1)} %collective-permute-done.1.got1, bf16[512,128]{1,0:T(8,128)(2,1)S(1)} %collective-permute-done.2.got2, ...), custom_call_target="tpu_custom_call" | custom-call | flops 1000000000 | bytes 1000000 | tf_op jit(solution)/shard_map/pallas_call | solution.py:269
Async XLA Ops:
  6.8 17.1 %collective-permute-start = (bf16[512,128]{1,0:T(8,128)(2,1)S(1)}, bf16[512,128]{1,0:T(8,128)(2,1)S(1)}, u32[]{:S(2)}, u32[]{:S(2)}) collective-permute-start(bf16[512,128]{1,0:T(8,128)(2,1)S(1)} %get-tuple-element.18), channel_id=1, source_target_pairs={{0,16},{32,48},{64,80},{96,112},{128,144},{160,176},{192,208},{224... | collective-permute-start | bytes 393224 | tf_op jit(solution)/shard_map/ppermute | solution.py:193
  8.7 15.2 %collective-permute-start.1 = (bf16[512,128]{1,0:T(8,128)(2,1)S(1)}, bf16[512,128]{1,0:T(8,128)(2,1)S(1)}, u32[]{:S(2)}, u32[]{:S(2)}) collective-permute-start(bf16[512,128]{1,0:T(8,128)(2,1)S(1)} %get-tuple-element.19), channel_id=1, source_target_pairs={{16,32},{48,64},{80,96},{112,128},{144,160},{176,192},{208,224},{2... | collective-permute-start | bytes 393224 | tf_op jit(solution)/shard_map/ppermute | solution.py:193
  15.9 8.0 %collective-permute-start.2 = (bf16[512,128]{1,0:T(8,128)(2,1)S(1)}, bf16[512,128]{1,0:T(8,128)(2,1)S(1)}, u32[]{:S(2)}, u32[]{:S(2)}) collective-permute-start(bf16[512,128]{1,0:T(8,128)(2,1)S(1)} %get-tuple-element.20), channel_id=1, source_target_pairs={{0,1},{2,3},{4,5},{6,7},{8,9},{10,11},{12,13},{14,15},{1,0},{3,2},... | collective-permute-start | bytes 393224 | tf_op jit(solution)/shard_map/ppermute | solution.py:193
  19.7 8.1 %collective-permute-start.3 = (bf16[512,128]{1,0:T(8,128)(2,1)S(1)}, bf16[512,128]{1,0:T(8,128)(2,1)S(1)}, u32[]{:S(2)}, u32[]{:S(2)}) collective-permute-start(bf16[512,128]{1,0:T(8,128)(2,1)S(1)} %get-tuple-element.21), channel_id=1, source_target_pairs={{1,2},{3,4},{5,6},{7,8},{9,10},{11,12},{13,14},{2,1},{4,3},{6,5},{... | collective-permute-start | bytes 393224 | tf_op jit(solution)/shard_map/ppermute | solution.py:193

commit v3 on v2

--- a/solution.py
+++ b/solution.py
@@ -13,6 +13,7 @@
 BF16 = jnp.bfloat16
 F32 = jnp.float32
 I32 = jnp.int32
+SLOTS = (3, 2, 1, 0)
 VMEM_LIMIT = 20 * 1024 * 1024
 
 
@@ -29,7 +30,8 @@
 def neighbor_order():
     blk_odd = lax.rem(lax.axis_index("blk"), 2)
     tile_odd = lax.rem(lax.axis_index("tile"), 2)
-    return (blk_odd, 1 - blk_odd, 2 + tile_odd, 3 - tile_odd)
+    sent = (blk_odd, 1 - blk_odd, 2 + tile_odd, 3 - tile_odd)
+    return [sent[kind] for kind in SLOTS]
 
 
 def mixing_matrix(vertical):
@@ -64,15 +66,17 @@
         part = slice(m * LANES, (m + 1) * LANES)
         rows = slice(m * 8, (m + 1) * 8)
         index = regroup(nb_ref[:, part])
-        code_ref[rows, :] = lax.div(index, LOW) * GROUP + (lane & (GROUP - 1))
-        low_ref[rows, :] = index & (LOW - 1)
+        code_ref[rows, :] = (lax.div(index, LOW) * GROUP + (lane & (GROUP - 1))).astype(F32)
+        low_ref[rows, :] = (index & (LOW - 1)).astype(F32)
         coeff_ref[rows, :] = regroup(cf_ref[:, part])
-    high_rows = iota((high_count * GROUP, LANES), 0)
-    low_rows = iota((LOW, LANES), 0)
+    high_rows = iota((high_count * GROUP, LANES), 0).astype(F32).astype(BF16)
+    low_rows = iota((LOW, LANES), 0).astype(F32).astype(BF16)
+    one, zero = jnp.ones((), BF16), jnp.zeros((), BF16)
     for g in range(points // GROUP):
-        high = jnp.where(high_rows == code_ref[g : g + 1, :], 1.0, 0.0).astype(BF16)
-        low = jnp.where(low_rows == low_ref[g : g + 1, :], coeff_ref[g : g + 1, :], 0.0)
-        out = dot(high, low.astype(BF16), 1, 1).astype(BF16)
+        code, low_row, coeff = (ref[g : g + 1, :].astype(BF16) for ref in (code_ref, low_ref, coeff_ref))
+        high = jnp.where(high_rows == code, one, zero)
+        low = jnp.where(low_rows == low_row, coeff, zero)
+        out = dot(high, low, 1, 1).astype(BF16)
         for h in range(high_count):
             s_ref[g * GROUP : (g + 1) * GROUP, h * LOW : (h + 1) * LOW] = out[
                 h * GROUP : (h + 1) * GROUP
@@ -83,11 +87,35 @@
     return jnp.where(iota((height, LANES), 0) == row, 1.0, 0.0).astype(BF16)
 
 
+def one_hot_rows(row, width):
+    column = jnp.broadcast_to(row.astype(F32), (LANES, LANES)).T
+    lane = iota((LANES, LANES), 1).astype(F32)
+    parts = [jnp.where(column == lane + float(c * LANES), 1.0, 0.0) for c in range(width // LANES)]
+    return jnp.concatenate([part.astype(BF16) for part in parts], axis=1)
+
+
+def send_selector(send_ref, slot, direction, points):
+    half = send_ref.shape[1]
+    first = SLOTS[slot] // 2 * 2
+    columns = []
+    for h in range(half // LANES):
+        lanes = slice(h * LANES, (h + 1) * LANES)
+        row = jnp.where(
+            direction == first, send_ref[first : first + 1, lanes], send_ref[first + 1 : first + 2, lanes]
+        )
+        columns.append(one_hot_columns(row, points))
+    return jnp.concatenate(columns, axis=1)
+
+
+def halo_part(ref, rows, direction, points, half):
+    return ref[rows, pl.ds(pl.multiple_of(points + (direction ^ 1) * half, half), half)]
+
+
 def adjoint_kernel(
     live_ref, field_hbm, send_hbm, nb_hbm, cf_hbm, vert_hbm, w_hbm, map_hbm, cot_hbm,
-    sent0, sent1, sent2, sent3, s_ref, pt_ref, mbt_ref, field_ref, send_ref, w_ref, mix_ref,
-    nb_ref, cf_ref, vert_ref, map_ref, cot_ref,
-    code_ref, low_ref, coeff_ref, bb_ref, back_ref, sems,
+    sent0, sent1, sent2, sent3, s_ref, mbt_ref, field_ref, send_ref, w_ref, mix_ref, map_ref,
+    nb_ref, cf_ref, vert_ref, cot_ref,
+    code_ref, low_ref, coeff_ref, p_ref, bbt_ref, back_ref, sems,
 ):
     order = neighbor_order()
     points = field_ref.shape[0]
@@ -107,66 +135,66 @@
     for copy in copies[2:]:
         copy.wait()
     for j in range(slots):
-        cols = slice(j * block, (j + 1) * block)
-        pt_ref[:, cols] = one_hot_columns(map_ref[j : j + 1, :], points)
-        result = dot(w_ref[j], cot_ref[cols, :], 0, 0)
-        bb_ref[cols, :] = jnp.where(j < live, result, 0.0).astype(BF16)
+        rows = slice(j * block, (j + 1) * block)
+        p_ref[rows, :] = one_hot_rows(map_ref[j : j + 1, :], points)
+        result = dot(cot_ref[rows, :], w_ref[j], 0, 0)
+        bbt_ref[:, rows] = jnp.where(j < live, result, 0.0).astype(BF16)
     mixing = mixing_matrix(vert_ref[...])
     mix_ref[...] = mixing.T.astype(BF16)
     for c in range(points // CHUNK):
-        rows = slice(c * CHUNK, (c + 1) * CHUNK)
-        back_ref[rows, :] = dot(pt_ref[rows, :], bb_ref[...]).astype(BF16)
-    mbt_ref[...] = dot(mixing.astype(BF16), back_ref[...], 1, 1).astype(BF16)
+        cols = slice(c * CHUNK, (c + 1) * CHUNK)
+        back_ref[:, cols] = dot(bbt_ref[...], p_ref[:, cols]).astype(BF16)
+    mbt_ref[...] = dot(mixing.astype(BF16), back_ref[...]).astype(BF16)
     field_t = field_ref[...].T
     for slot, sent in enumerate((sent0, sent1, sent2, sent3)):
-        columns = []
-        for h in range(half // LANES):
-            lanes = slice(h * LANES, (h + 1) * LANES)
-            first = slot // 2 * 2
-            row = jnp.where(
-                order[slot] == first, send_ref[first : first + 1, lanes], send_ref[first + 1 : first + 2, lanes]
-            )
-            columns.append(one_hot_columns(row, points))
-        sent[:half, :] = dot(field_t, jnp.concatenate(columns, axis=1)).T.astype(BF16)
-        start = pl.multiple_of(points + (order[slot] ^ 1) * half, half)
-        sent[half:, :] = dot(mbt_ref[...], s_ref[:, pl.ds(start, half)]).T.astype(BF16)
-
-
-def local_kernel(mbt_ref, s_ref, field_ref, send_ref, own_ref, hor_ref, sel_ref):
+        sent[:half, :] = dot(field_t, send_selector(send_ref, slot, order[slot], points)).T.astype(BF16)
+        part = halo_part(s_ref, slice(None), order[slot], points, half)
+        sent[half:, :] = dot(mbt_ref[...], part).T.astype(BF16)
+
+
+def local_kernel(
+    got0, got1, mbt_ref, s_ref, field_ref, send_ref, map_ref, own_ref, hor_ref, sel_ref, pt_ref, tile_ref
+):
+    order = neighbor_order()
     points = field_ref.shape[0]
     half = send_ref.shape[1]
+    slots, block = map_ref.shape
+    for slot in range(4):
+        target = tile_ref if slot < 2 else sel_ref
+        start = slot % 2 * half
+        target[:, start : start + half] = send_selector(send_ref, slot, order[slot], points)
+    for j in range(slots):
+        pt_ref[:, j * block : (j + 1) * block] = one_hot_columns(map_ref[j : j + 1, :], points)
     for c in range(points // CHUNK):
         rows = slice(c * CHUNK, (c + 1) * CHUNK)
-        own_ref[rows, :] = dot(mbt_ref[...], s_ref[:, rows]).T
-        hor_ref[rows, :] = dot(s_ref[rows, :points], field_ref[...])
-    for q in range(4):
-        for h in range(half // LANES):
-            cols = slice(q * half + h * LANES, q * half + (h + 1) * LANES)
-            row = send_ref[q : q + 1, h * LANES : (h + 1) * LANES]
-            sel_ref[:, cols] = one_hot_columns(row, points)
+        own = dot(mbt_ref[...], s_ref[:, rows]).T
+        own = own + dot(tile_ref[rows, :half], got0[half:, :])
+        own_ref[rows, :] = own + dot(tile_ref[rows, half:], got1[half:, :])
+        hor = dot(s_ref[rows, :points], field_ref[...])
+        hor = hor + dot(halo_part(s_ref, rows, order[0], points, half), got0[:half, :])
+        hor_ref[rows, :] = hor + dot(halo_part(s_ref, rows, order[1], points, half), got1[:half, :])
 
 
 def forward_kernel(
-    live_ref, got0, got1, got2, got3, s_ref, pt_ref, w_ref, mix_ref, own_ref, hor_ref, sel_ref,
+    live_ref, got2, got3, s_ref, pt_ref, w_ref, mix_ref, own_ref, hor_ref, sel_ref,
     grid_hbm, grad_hbm,
-    halo_ref, ret_ref, hb_ref, conv_ref, src_ref, grid_ref, grad_ref, sems,
+    hb_ref, conv_ref, src_ref, grid_ref, grad_ref, sems,
 ):
     order = neighbor_order()
     points = hor_ref.shape[0]
-    half = got0.shape[0] // 2
+    half = got2.shape[0] // 2
     slots, block = w_ref.shape[0], w_ref.shape[1]
     live = live_ref[0, 0]
-    for slot, got in enumerate((got0, got1, got2, got3)):
-        start = pl.multiple_of((order[slot] ^ 1) * half, half)
-        halo_ref[pl.ds(start, half), :] = got[:half, :]
-        ret_ref[pl.ds(pl.multiple_of(order[slot] * half, half), half), :] = got[half:, :]
     for c in range(points // CHUNK):
         rows = slice(c * CHUNK, (c + 1) * CHUNK)
-        hb_ref[rows, :] = (hor_ref[rows, :] + dot(s_ref[rows, points:], halo_ref[...])).astype(BF16)
+        hor = hor_ref[rows, :] + dot(halo_part(s_ref, rows, order[2], points, half), got2[:half, :])
+        hor = hor + dot(halo_part(s_ref, rows, order[3], points, half), got3[:half, :])
+        hb_ref[rows, :] = hor.astype(BF16)
     conv_ref[...] = dot(mix_ref[...], hb_ref[...], 1, 1).astype(BF16)
     for c in range(points // CHUNK):
         rows = slice(c * CHUNK, (c + 1) * CHUNK)
-        grad_ref[rows, :] = (own_ref[rows, :] + dot(sel_ref[rows, :], ret_ref[...])).astype(BF16)
+        own = own_ref[rows, :] + dot(sel_ref[rows, :half], got2[half:, :])
+        grad_ref[rows, :] = (own + dot(sel_ref[rows, half:], got3[half:, :])).astype(BF16)
     copies = [pltpu.make_async_copy(grad_ref, grad_hbm, sems.at[0])]
     copies[0].start()
     for c in range(slots * block // CHUNK):
@@ -222,14 +250,14 @@
     params = pltpu.CompilerParams(vmem_limit_bytes=VMEM_LIMIT)
     shared = (
         pltpu.VMEM((points, width), BF16),
-        pltpu.VMEM((points, slots * block), BF16),
         pltpu.VMEM((feat, points), BF16),
         pltpu.VMEM(field.shape, BF16),
         pltpu.VMEM(send.shape, I32),
         pltpu.VMEM(weights.shape, BF16),
         pltpu.VMEM((feat, feat), BF16),
+        pltpu.VMEM(mapped.shape, I32),
     )
-    sent0, sent1, sent2, sent3, s_mat, pt_mat, mbt, field_v, send_v, w_v, mix = pl.pallas_call(
+    sent0, sent1, sent2, sent3, s_mat, mbt, field_v, send_v, w_v, mix, map_v = pl.pallas_call(
         adjoint_kernel,
         out_shape=(pltpu.VMEM((2 * half, feat), BF16),) * 4 + shared,
         in_specs=[smem] + [hbm] * 8,
@@ -238,45 +266,45 @@
             pltpu.VMEM(nb.shape, I32),
             pltpu.VMEM(cf.shape, F32),
             pltpu.VMEM(vert.shape, F32),
-            pltpu.VMEM(mapped.shape, I32),
             pltpu.VMEM(cotangent.shape, BF16),
-            pltpu.VMEM((points // GROUP, LANES), I32),
-            pltpu.VMEM((points // GROUP, LANES), I32),
             pltpu.VMEM((points // GROUP, LANES), F32),
-            pltpu.VMEM((slots * block, feat), BF16),
-            pltpu.VMEM((points, feat), BF16),
+            pltpu.VMEM((points // GROUP, LANES), F32),
+            pltpu.VMEM((points // GROUP, LANES), F32),
+            pltpu.VMEM((slots * block, points), BF16),
+            pltpu.VMEM((feat, slots * block), BF16),
+            pltpu.VMEM((feat, points), BF16),
             pltpu.SemaphoreType.DMA((8,)),
         ],
         compiler_params=params,
         cost_estimate=cost(2 * 10**9),
     )(tally, *in_hbm(field, send, nb, cf, vert, weights, mapped, cotangent))
-    got0 = exchange(sent0, "blk", 0, True)
-    got1 = exchange(sent1, "blk", 1, True)
-    got2 = exchange(sent2, "tile", 0, False)
-    got3 = exchange(sent3, "tile", 1, False)
-    own, hor, sel = pl.pallas_call(
+    got0, got1, got2, got3 = (
+        exchange(sent, ("blk", "tile")[kind // 2], kind % 2, kind < 2)
+        for kind, sent in zip(SLOTS, (sent0, sent1, sent2, sent3))
+    )
+    own, hor, sel, pt_mat = pl.pallas_call(
         local_kernel,
         out_shape=(
             pltpu.VMEM((points, feat), F32),
             pltpu.VMEM((points, feat), F32),
-            pltpu.VMEM((points, 4 * half), BF16),
+            pltpu.VMEM((points, 2 * half), BF16),
+            pltpu.VMEM((points, slots * block), BF16),
         ),
-        in_specs=[vmem] * 4,
-        out_specs=(vmem,) * 3,
+        in_specs=[vmem] * 7,
+        out_specs=(vmem,) * 4,
+        scratch_shapes=[pltpu.VMEM((points, 2 * half), BF16)],
         compiler_params=params,
         cost_estimate=cost(10**9),
-    )(*in_vmem(mbt, s_mat, field_v, send_v))
+    )(*in_vmem(got0, got1, mbt, s_mat, field_v, send_v, map_v))
     grid, grad = pl.pallas_call(
         forward_kernel,
         out_shape=(
             pltpu.HBM((slots * block, feat), BF16),
             pltpu.HBM((points, feat), BF16),
         ),
-        in_specs=[smem] + [vmem] * 11,
+        in_specs=[smem] + [vmem] * 9,
         out_specs=(hbm, hbm),
         scratch_shapes=[
-            pltpu.VMEM((4 * half, feat), BF16),
-            pltpu.VMEM((4 * half, feat), BF16),
             pltpu.VMEM((points, feat), BF16),
             pltpu.VMEM((feat, points), BF16),
             pltpu.VMEM((slots * block, feat), BF16),
@@ -286,7 +314,7 @@
         ],
         compiler_params=params,
         cost_estimate=cost(10**9),
-    )(tally, *in_vmem(got0, got1, got2, got3, s_mat, pt_mat, w_v, mix, own, hor, sel))
+    )(tally, *in_vmem(got2, got3, s_mat, pt_mat, w_v, mix, own, hor, sel))
     return grid[None, None], grad[None, None]
 
 

time: 31 us -> 28.4 us (0.916)
  the two profiles are of different devices: /device:TPU:128 before, /device:TPU:65 now
where the time goes in v3:
time: 28.4 us; the launch traced here: 28.2 us
  starting transfers between devices  17.4 us (61%)
  Pallas kernels  9.35 us (33%)
  between operations  1.36 us (5%)
    ppermute x4, starting transfers between devices, exchange(): return lax.ppermute(value, axis, pairs + [(b, a) for a, b in pairs])  17.4 us
    pallas_call x1, Pallas kernels, shards(): pl.pallas_call(adjoint_kernel, out_shape=(pltpu.VMEM((2 * half, feat), BF...  4.23 us
    pallas_call x1, Pallas kernels, shards(): pl.pallas_call(local_kernel, out_shape=(pltpu.VMEM((points, feat), F32),...  2.61 us
    pallas_call x1, Pallas kernels, shards(): pl.pallas_call(forward_kernel, out_shape=(pltpu.HBM((slots * block, feat)...  2.51 us
  transfers between devices with their start and end apart: 4, of which 0 were waited for; matrix products, arithmetic and copies ran while one was open for 0% of the time, Pallas kernels for 9%

profile of v3, /device:TPU:65, one launch (start us, length us, event | category | flops | bytes accessed | tf_op | source)
XLA Modules:
  0.0 28.2 jit_solution(16547726135211970143)
XLA Ops:
  1.3 4.2 %shard_map.104 = (bf16[512,128]{1,0:T(8,128)(2,1)S(1)}, bf16[512,128]{1,0:T(8,128)(2,1)S(1)}, bf16[512,128]{1,0:T(8,128)(2,1)S(1)}, bf16[512,128]{1,0:T(8,128)(2...) custom-call(s32[1,1]{1,0:T(1,128)S(6)} %copy.11.live_ref, ...), custom_call_target="tpu_custom_call" | custom-call | flops 2000000000 | bytes 1000000 | tf_op jit(solution)/shard_map/pallas_call | solution.py:260
  5.5 1.9 %collective-permute-start.2 = (bf16[512,128]{1,0:T(8,128)(2,1)S(1)}, bf16[512,128]{1,0:T(8,128)(2,1)S(1)}, u32[]{:S(2)}, u32[]{:S(2)}) collective-permute-start(bf16[512,128]{1,0:T(8,128)(2,1)S(1)} %get-tuple-element.22), channel_id=1, source_target_pairs={{1,2},{3,4},{5,6},{7,8},{9,10},{11,12},{13,14},{2,1},{4,3},{6,5},{... | collective-permute-start | bytes 393224 | tf_op jit(solution)/shard_map/ppermute | solution.py:221
  7.4 6.4 %collective-permute-start.3 = (bf16[512,128]{1,0:T(8,128)(2,1)S(1)}, bf16[512,128]{1,0:T(8,128)(2,1)S(1)}, u32[]{:S(2)}, u32[]{:S(2)}) collective-permute-start(bf16[512,128]{1,0:T(8,128)(2,1)S(1)} %get-tuple-element.23), channel_id=1, source_target_pairs={{0,1},{2,3},{4,5},{6,7},{8,9},{10,11},{12,13},{14,15},{1,0},{3,2},... | collective-permute-start | bytes 393224 | tf_op jit(solution)/shard_map/ppermute | solution.py:221
  13.8 4.3 %collective-permute-start = (bf16[512,128]{1,0:T(8,128)(2,1)S(1)}, bf16[512,128]{1,0:T(8,128)(2,1)S(1)}, u32[]{:S(2)}, u32[]{:S(2)}) collective-permute-start(bf16[512,128]{1,0:T(8,128)(2,1)S(1)} %get-tuple-element.19), channel_id=1, source_target_pairs={{16,32},{48,64},{80,96},{112,128},{144,160},{176,192},{208,224},{2... | collective-permute-start | bytes 393224 | tf_op jit(solution)/shard_map/ppermute | solution.py:221
  18.2 4.8 %collective-permute-start.1 = (bf16[512,128]{1,0:T(8,128)(2,1)S(1)}, bf16[512,128]{1,0:T(8,128)(2,1)S(1)}, u32[]{:S(2)}, u32[]{:S(2)}) collective-permute-start(bf16[512,128]{1,0:T(8,128)(2,1)S(1)} %get-tuple-element.20), channel_id=1, source_target_pairs={{0,16},{32,48},{64,80},{96,112},{128,144},{160,176},{192,208},{224... | collective-permute-start | bytes 393224 | tf_op jit(solution)/shard_map/ppermute | solution.py:221
  23.0 0.0 collective-permute-done.2.got0
  23.0 0.0 collective-permute-done.3.got1
  23.0 2.6 %shard_map.105 = (f32[1024,128]{1,0:T(8,128)S(1)}, f32[1024,128]{1,0:T(8,128)S(1)}, bf16[1024,512]{1,0:T(8,128)(2,1)S(1)}, bf16[1024,2048]{1,0:T(8,128)(2,1)S(1)}) custom-call(bf16[512,128]{1,0:T(8,128)(2,1)S(1)} %collective-permute-done.2.got0, bf16[512,128]{1,0:T(8,128)(2,1)S(1)} %collective-permute-done.3.got1, ...), custom_call_target="tpu_custom_call" | custom-call | flops 1000000000 | bytes 1000000 | tf_op jit(solution)/shard_map/pallas_call | solution.py:285
  25.6 0.0 collective-permute-done.got2
  25.6 0.0 collective-permute-done.1.got3
  25.6 2.5 %shard_map.106 = (bf16[2048,128]{1,0:T(8,128)(2,1)}, bf16[1024,128]{1,0:T(8,128)(2,1)}) custom-call(s32[1,1]{1,0:T(1,128)S(6)} %copy.11.live_ref, bf16[512,128]{1,0:T(8,128)(2,1)S(1)} %collective-permute-done.got2, bf16[512,128]{1,0:T(8,128)(2,1)S(1)} %collective-permute-done.1.got3, bf16[1024,2048]{1,0:T(8,128)(2,1)S(1)} %get-tuple-element.21.s_ref, ...), custom_call_target="tpu_custom_call" | custom-call | flops 1000000000 | bytes 1000000 | tf_op jit(solution)/shard_map/pallas_call | solution.py:299
Async XLA Ops:
  5.5 17.5 %collective-permute-start.2 = (bf16[512,128]{1,0:T(8,128)(2,1)S(1)}, bf16[512,128]{1,0:T(8,128)(2,1)S(1)}, u32[]{:S(2)}, u32[]{:S(2)}) collective-permute-start(bf16[512,128]{1,0:T(8,128)(2,1)S(1)} %get-tuple-element.22), channel_id=1, source_target_pairs={{1,2},{3,4},{5,6},{7,8},{9,10},{11,12},{13,14},{2,1},{4,3},{6,5},{... | collective-permute-start | bytes 393224 | tf_op jit(solution)/shard_map/ppermute | solution.py:221
  7.4 15.6 %collective-permute-start.3 = (bf16[512,128]{1,0:T(8,128)(2,1)S(1)}, bf16[512,128]{1,0:T(8,128)(2,1)S(1)}, u32[]{:S(2)}, u32[]{:S(2)}) collective-permute-start(bf16[512,128]{1,0:T(8,128)(2,1)S(1)} %get-tuple-element.23), channel_id=1, source_target_pairs={{0,1},{2,3},{4,5},{6,7},{8,9},{10,11},{12,13},{14,15},{1,0},{3,2},... | collective-permute-start | bytes 393224 | tf_op jit(solution)/shard_map/ppermute | solution.py:221
  13.8 11.8 %collective-permute-start = (bf16[512,128]{1,0:T(8,128)(2,1)S(1)}, bf16[512,128]{1,0:T(8,128)(2,1)S(1)}, u32[]{:S(2)}, u32[]{:S(2)}) collective-permute-start(bf16[512,128]{1,0:T(8,128)(2,1)S(1)} %get-tuple-element.19), channel_id=1, source_target_pairs={{16,32},{48,64},{80,96},{112,128},{144,160},{176,192},{208,224},{2... | collective-permute-start | bytes 393224 | tf_op jit(solution)/shard_map/ppermute | solution.py:221
  18.2 7.5 %collective-permute-start.1 = (bf16[512,128]{1,0:T(8,128)(2,1)S(1)}, bf16[512,128]{1,0:T(8,128)(2,1)S(1)}, u32[]{:S(2)}, u32[]{:S(2)}) collective-permute-start(bf16[512,128]{1,0:T(8,128)(2,1)S(1)} %get-tuple-element.20), channel_id=1, source_target_pairs={{0,16},{32,48},{64,80},{96,112},{128,144},{160,176},{192,208},{224... | collective-permute-start | bytes 393224 | tf_op jit(solution)/shard_map/ppermute | solution.py:221

commit v4 on v3

--- a/solution.py
+++ b/solution.py
@@ -14,6 +14,7 @@
 F32 = jnp.float32
 I32 = jnp.int32
 SLOTS = (3, 2, 1, 0)
+ROW = 8
 VMEM_LIMIT = 20 * 1024 * 1024
 
 
@@ -152,7 +153,20 @@
         sent[half:, :] = dot(mbt_ref[...], part).T.astype(BF16)
 
 
-def local_kernel(
+def far_neighbor():
+    place = lax.rem(lax.axis_index("blk"), ROW)
+    return jnp.logical_or(place == 0, place == ROW - 1)
+
+
+def early_kernel(*refs):
+    pl.when(jnp.logical_not(far_neighbor()))(lambda: local_work(*refs[:7], *refs[8:12], refs[13]))
+
+
+def late_kernel(*refs):
+    pl.when(far_neighbor())(lambda: local_work(*refs[:7], *refs[11:]))
+
+
+def local_work(
     got0, got1, mbt_ref, s_ref, field_ref, send_ref, map_ref, own_ref, hor_ref, sel_ref, pt_ref, tile_ref
 ):
     order = neighbor_order()
@@ -163,8 +177,16 @@
         target = tile_ref if slot < 2 else sel_ref
         start = slot % 2 * half
         target[:, start : start + half] = send_selector(send_ref, slot, order[slot], points)
-    for j in range(slots):
-        pt_ref[:, j * block : (j + 1) * block] = one_hot_columns(map_ref[j : j + 1, :], points)
+    index = map_ref[...]
+    low = (index & (LANES - 1)).astype(F32).astype(BF16)
+    high = lax.div(index, LANES)
+    row_ids = iota((LANES, LANES), 0).astype(F32).astype(BF16)
+    for p in range(points // LANES):
+        here = jnp.where(high == p, 1.0, 0.0).astype(BF16)
+        for j in range(slots):
+            pt_ref[p * LANES : (p + 1) * LANES, j * block : (j + 1) * block] = jnp.where(
+                row_ids == low[j : j + 1], here[j : j + 1], jnp.zeros((), BF16)
+            )
     for c in range(points // CHUNK):
         rows = slice(c * CHUNK, (c + 1) * CHUNK)
         own = dot(mbt_ref[...], s_ref[:, rows]).T
@@ -278,24 +300,39 @@
         compiler_params=params,
         cost_estimate=cost(2 * 10**9),
     )(tally, *in_hbm(field, send, nb, cf, vert, weights, mapped, cotangent))
-    got0, got1, got2, got3 = (
-        exchange(sent, ("blk", "tile")[kind // 2], kind % 2, kind < 2)
-        for kind, sent in zip(SLOTS, (sent0, sent1, sent2, sent3))
+    def trade(slot, sent):
+        kind = SLOTS[slot]
+        return exchange(sent, ("blk", "tile")[kind // 2], kind % 2, kind < 2)
+
+    got0, got1, got2 = trade(0, sent0), trade(1, sent1), trade(2, sent2)
+    local_shapes = (
+        pltpu.VMEM((points, feat), F32),
+        pltpu.VMEM((points, feat), F32),
+        pltpu.VMEM((points, 2 * half), BF16),
+        pltpu.VMEM((points, slots * block), BF16),
     )
+    shared = (got0, got1, mbt, s_mat, field_v, send_v, map_v)
+    *local, sent3 = pl.pallas_call(
+        early_kernel,
+        out_shape=local_shapes + (pltpu.VMEM(sent3.shape, BF16),),
+        in_specs=[vmem] * 8,
+        out_specs=(vmem,) * 5,
+        scratch_shapes=[pltpu.VMEM((points, 2 * half), BF16)],
+        input_output_aliases={7: 4},
+        compiler_params=params,
+        cost_estimate=cost(10**9),
+    )(*in_vmem(*shared, sent3))
+    got3 = trade(3, sent3)
     own, hor, sel, pt_mat = pl.pallas_call(
-        local_kernel,
-        out_shape=(
-            pltpu.VMEM((points, feat), F32),
-            pltpu.VMEM((points, feat), F32),
-            pltpu.VMEM((points, 2 * half), BF16),
-            pltpu.VMEM((points, slots * block), BF16),
-        ),
-        in_specs=[vmem] * 7,
+        late_kernel,
+        out_shape=local_shapes,
+        in_specs=[vmem] * 11,
         out_specs=(vmem,) * 4,
         scratch_shapes=[pltpu.VMEM((points, 2 * half), BF16)],
+        input_output_aliases={7 + i: i for i in range(4)},
         compiler_params=params,
         cost_estimate=cost(10**9),
-    )(*in_vmem(got0, got1, mbt, s_mat, field_v, send_v, map_v))
+    )(*in_vmem(*shared, *local))
     grid, grad = pl.pallas_call(
         forward_kernel,
         out_shape=(

time: 28.4 us -> 27.4 us (0.965)
  the two profiles are of different devices: /device:TPU:65 before, /device:TPU:221 now
where the time goes in v4:
time: 27.4 us; the launch traced here: 27.2 us
  starting transfers between devices  16.8 us (61%)
  Pallas kernels  9.01 us (33%)
  between operations  1.37 us (5%)
    ppermute x4, starting transfers between devices, exchange(): return lax.ppermute(value, axis, pairs + [(b, a) for a, b in pairs])  16.8 us
    pallas_call x1, Pallas kernels, shards(): pl.pallas_call(adjoint_kernel, out_shape=(pltpu.VMEM((2 * half, feat), BF...  4.23 us
    pallas_call x1, Pallas kernels, shards(): pl.pallas_call(forward_kernel, out_shape=(pltpu.HBM((slots * block, feat)...  2.53 us
    pallas_call x1, Pallas kernels, shards(): pl.pallas_call(late_kernel, out_shape=local_shapes, in_specs=[vmem] * 11,...  2.24 us
  transfers between devices with their start and end apart: 4, of which 0 were waited for; matrix products, arithmetic and copies ran while one was open for 0% of the time, Pallas kernels for 8%

profile of v4, /device:TPU:221, one launch (start us, length us, event | category | flops | bytes accessed | tf_op | source)
XLA Modules:
  0.0 27.2 jit_solution(8648481694453946320)
XLA Ops:
  1.3 4.2 %shard_map.104 = (bf16[512,128]{1,0:T(8,128)(2,1)S(1)}, bf16[512,128]{1,0:T(8,128)(2,1)S(1)}, bf16[512,128]{1,0:T(8,128)(2,1)S(1)}, bf16[512,128]{1,0:T(8,128)(2...) custom-call(s32[1,1]{1,0:T(1,128)S(6)} %copy.21.live_ref, ...), custom_call_target="tpu_custom_call" | custom-call | flops 2000000000 | bytes 1000000 | tf_op jit(solution)/shard_map/pallas_call | solution.py:282
  5.5 1.9 %collective-permute-start.1 = (bf16[512,128]{1,0:T(8,128)(2,1)S(1)}, bf16[512,128]{1,0:T(8,128)(2,1)S(1)}, u32[]{:S(2)}, u32[]{:S(2)}) collective-permute-start(bf16[512,128]{1,0:T(8,128)(2,1)S(1)} %get-tuple-element.25), channel_id=1, source_target_pairs={{1,2},{3,4},{5,6},{7,8},{9,10},{11,12},{13,14},{2,1},{4,3},{6,5},{... | collective-permute-start | bytes 393224 | tf_op jit(solution)/shard_map/ppermute | solution.py:243
  7.4 6.4 %collective-permute-start.2 = (bf16[512,128]{1,0:T(8,128)(2,1)S(1)}, bf16[512,128]{1,0:T(8,128)(2,1)S(1)}, u32[]{:S(2)}, u32[]{:S(2)}) collective-permute-start(bf16[512,128]{1,0:T(8,128)(2,1)S(1)} %get-tuple-element.26), channel_id=1, source_target_pairs={{0,1},{2,3},{4,5},{6,7},{8,9},{10,11},{12,13},{14,15},{1,0},{3,2},... | collective-permute-start | bytes 393224 | tf_op jit(solution)/shard_map/ppermute | solution.py:243
  13.8 3.6 %collective-permute-start = (bf16[512,128]{1,0:T(8,128)(2,1)S(1)}, bf16[512,128]{1,0:T(8,128)(2,1)S(1)}, u32[]{:S(2)}, u32[]{:S(2)}) collective-permute-start(bf16[512,128]{1,0:T(8,128)(2,1)S(1)} %get-tuple-element.24), channel_id=1, source_target_pairs={{16,32},{48,64},{80,96},{112,128},{144,160},{176,192},{208,224},{2... | collective-permute-start | bytes 393224 | tf_op jit(solution)/shard_map/ppermute | solution.py:243
  17.4 0.0 collective-permute-done.1.refs_0_
  17.5 0.0 collective-permute-done.2.refs_1_
  17.5 4.9 %collective-permute-start.3 = (bf16[512,128]{1,0:T(8,128)(2,1)S(1)}, bf16[512,128]{1,0:T(8,128)(2,1)S(1)}, u32[]{:S(2)}, u32[]{:S(2)}) collective-permute-start(bf16[512,128]{1,0:T(8,128)(2,1)S(1)} %get-tuple-element.33), channel_id=1, source_target_pairs={{0,16},{32,48},{64,80},{96,112},{128,144},{160,176},{192,208},{224... | collective-permute-start | bytes 393224 | tf_op jit(solution)/shard_map/ppermute | solution.py:243
  22.4 2.2 %shard_map.106 = (f32[1024,128]{1,0:T(8,128)S(1)}, f32[1024,128]{1,0:T(8,128)S(1)}, bf16[1024,512]{1,0:T(8,128)(2,1)S(1)}, bf16[1024,2048]{1,0:T(8,128)(2,1)S(1)}) custom-call(bf16[512,128]{1,0:T(8,128)(2,1)S(1)} %collective-permute-done.1.refs_0_, ...), custom_call_target="tpu_custom_call", output_to_operand_aliasing={{0}: (7, {}), {1}: (8, {}), {2}: (9, {}), {3}: (10, {})} | custom-call | flops 1000000000 | bytes 1000000 | tf_op jit(solution)/shard_map/pallas_call | solution.py:326
  24.7 0.0 collective-permute-done.got2
  24.7 0.0 collective-permute-done.3.got3
  24.7 2.5 %shard_map.107 = (bf16[2048,128]{1,0:T(8,128)(2,1)}, bf16[1024,128]{1,0:T(8,128)(2,1)}) custom-call(s32[1,1]{1,0:T(1,128)S(6)} %copy.21.live_ref, bf16[512,128]{1,0:T(8,128)(2,1)S(1)} %collective-permute-done.got2, bf16[512,128]{1,0:T(8,128)(2,1)S(1)} %collective-permute-done.3.got3, bf16[1024,2048]{1,0:T(8,128)(2,1)S(1)} %get-tuple-element.28.refs_3_.s_ref, ...), custom_call_target="tpu_custom_call" | custom-call | flops 1000000000 | bytes 1000000 | tf_op jit(solution)/shard_map/pallas_call | solution.py:336
  (1 shorter events, 0.0 us)
Async XLA Ops:
  5.5 11.9 %collective-permute-start.1 = (bf16[512,128]{1,0:T(8,128)(2,1)S(1)}, bf16[512,128]{1,0:T(8,128)(2,1)S(1)}, u32[]{:S(2)}, u32[]{:S(2)}) collective-permute-start(bf16[512,128]{1,0:T(8,128)(2,1)S(1)} %get-tuple-element.25), channel_id=1, source_target_pairs={{1,2},{3,4},{5,6},{7,8},{9,10},{11,12},{13,14},{2,1},{4,3},{6,5},{... | collective-permute-start | bytes 393224 | tf_op jit(solution)/shard_map/ppermute | solution.py:243
  7.4 10.0 %collective-permute-start.2 = (bf16[512,128]{1,0:T(8,128)(2,1)S(1)}, bf16[512,128]{1,0:T(8,128)(2,1)S(1)}, u32[]{:S(2)}, u32[]{:S(2)}) collective-permute-start(bf16[512,128]{1,0:T(8,128)(2,1)S(1)} %get-tuple-element.26), channel_id=1, source_target_pairs={{0,1},{2,3},{4,5},{6,7},{8,9},{10,11},{12,13},{14,15},{1,0},{3,2},... | collective-permute-start | bytes 393224 | tf_op jit(solution)/shard_map/ppermute | solution.py:243
  13.8 10.8 %collective-permute-start = (bf16[512,128]{1,0:T(8,128)(2,1)S(1)}, bf16[512,128]{1,0:T(8,128)(2,1)S(1)}, u32[]{:S(2)}, u32[]{:S(2)}) collective-permute-start(bf16[512,128]{1,0:T(8,128)(2,1)S(1)} %get-tuple-element.24), channel_id=1, source_target_pairs={{16,32},{48,64},{80,96},{112,128},{144,160},{176,192},{208,224},{2... | collective-permute-start | bytes 393224 | tf_op jit(solution)/shard_map/ppermute | solution.py:243
  17.5 7.2 %collective-permute-start.3 = (bf16[512,128]{1,0:T(8,128)(2,1)S(1)}, bf16[512,128]{1,0:T(8,128)(2,1)S(1)}, u32[]{:S(2)}, u32[]{:S(2)}) collective-permute-start(bf16[512,128]{1,0:T(8,128)(2,1)S(1)} %get-tuple-element.33), channel_id=1, source_target_pairs={{0,16},{32,48},{64,80},{96,112},{128,144},{160,176},{192,208},{224... | collective-permute-start | bytes 393224 | tf_op jit(solution)/shard_map/ppermute | solution.py:243

commit v5 on v4

--- a/solution.py
+++ b/solution.py
@@ -14,7 +14,6 @@
 F32 = jnp.float32
 I32 = jnp.int32
 SLOTS = (3, 2, 1, 0)
-ROW = 8
 VMEM_LIMIT = 20 * 1024 * 1024
 
 
@@ -154,8 +153,7 @@
 
 
 def far_neighbor():
-    place = lax.rem(lax.axis_index("blk"), ROW)
-    return jnp.logical_or(place == 0, place == ROW - 1)
+    return lax.axis_index("blk") == 0
 
 
 def early_kernel(*refs):

time: 27.4 us -> 27.4 us (level)
  the two profiles are of different devices: /device:TPU:221 before, /device:TPU:64 now
where the time goes in v5:
time: 27.4 us; the launch traced here: 27.1 us
  starting transfers between devices  16.8 us (61%)
  Pallas kernels  8.99 us (33%)
  between operations  1.37 us (5%)
    ppermute x4, starting transfers between devices, exchange(): return lax.ppermute(value, axis, pairs + [(b, a) for a, b in pairs])  16.8 us
    pallas_call x1, Pallas kernels, shards(): pl.pallas_call(adjoint_kernel, out_shape=(pltpu.VMEM((2 * half, feat), BF...  4.23 us
    pallas_call x1, Pallas kernels, shards(): pl.pallas_call(forward_kernel, out_shape=(pltpu.HBM((slots * block, feat)...  2.51 us
    pallas_call x1, Pallas kernels, shards(): pl.pallas_call(late_kernel, out_shape=local_shapes, in_specs=[vmem] * 11,...  2.23 us
  transfers between devices with their start and end apart: 4, of which 0 were waited for; matrix products, arithmetic and copies ran while one was open for 0% of the time, Pallas kernels for 8%

profile of v5, /device:TPU:64, one launch (start us, length us, event | category | flops | bytes accessed | tf_op | source)
XLA Modules:
  0.0 27.1 jit_solution(7120986690025163833)
XLA Ops:
  1.3 4.2 %shard_map.104 = (bf16[512,128]{1,0:T(8,128)(2,1)S(1)}, bf16[512,128]{1,0:T(8,128)(2,1)S(1)}, bf16[512,128]{1,0:T(8,128)(2,1)S(1)}, bf16[512,128]{1,0:T(8,128)(2...) custom-call(s32[1,1]{1,0:T(1,128)S(6)} %copy.21.live_ref, ...), custom_call_target="tpu_custom_call" | custom-call | flops 2000000000 | bytes 1000000 | tf_op jit(solution)/shard_map/pallas_call | solution.py:280
  5.5 2.0 %collective-permute-start.1 = (bf16[512,128]{1,0:T(8,128)(2,1)S(1)}, bf16[512,128]{1,0:T(8,128)(2,1)S(1)}, u32[]{:S(2)}, u32[]{:S(2)}) collective-permute-start(bf16[512,128]{1,0:T(8,128)(2,1)S(1)} %get-tuple-element.25), channel_id=1, source_target_pairs={{1,2},{3,4},{5,6},{7,8},{9,10},{11,12},{13,14},{2,1},{4,3},{6,5},{... | collective-permute-start | bytes 393224 | tf_op jit(solution)/shard_map/ppermute | solution.py:241
  7.5 6.8 %collective-permute-start.2 = (bf16[512,128]{1,0:T(8,128)(2,1)S(1)}, bf16[512,128]{1,0:T(8,128)(2,1)S(1)}, u32[]{:S(2)}, u32[]{:S(2)}) collective-permute-start(bf16[512,128]{1,0:T(8,128)(2,1)S(1)} %get-tuple-element.26), channel_id=1, source_target_pairs={{0,1},{2,3},{4,5},{6,7},{8,9},{10,11},{12,13},{14,15},{1,0},{3,2},... | collective-permute-start | bytes 393224 | tf_op jit(solution)/shard_map/ppermute | solution.py:241
  14.4 6.0 %collective-permute-start = (bf16[512,128]{1,0:T(8,128)(2,1)S(1)}, bf16[512,128]{1,0:T(8,128)(2,1)S(1)}, u32[]{:S(2)}, u32[]{:S(2)}) collective-permute-start(bf16[512,128]{1,0:T(8,128)(2,1)S(1)} %get-tuple-element.24), channel_id=1, source_target_pairs={{16,32},{48,64},{80,96},{112,128},{144,160},{176,192},{208,224},{2... | collective-permute-start | bytes 393224 | tf_op jit(solution)/shard_map/ppermute | solution.py:241
  20.4 0.0 collective-permute-done.1.refs_0_
  20.4 0.0 collective-permute-done.2.refs_1_
  20.4 1.9 %collective-permute-start.3 = (bf16[512,128]{1,0:T(8,128)(2,1)S(1)}, bf16[512,128]{1,0:T(8,128)(2,1)S(1)}, u32[]{:S(2)}, u32[]{:S(2)}) collective-permute-start(bf16[512,128]{1,0:T(8,128)(2,1)S(1)} %get-tuple-element.33), channel_id=1, source_target_pairs={{0,16},{32,48},{64,80},{96,112},{128,144},{160,176},{192,208},{224... | collective-permute-start | bytes 393224 | tf_op jit(solution)/shard_map/ppermute | solution.py:241
  22.4 2.2 %shard_map.106 = (f32[1024,128]{1,0:T(8,128)S(1)}, f32[1024,128]{1,0:T(8,128)S(1)}, bf16[1024,512]{1,0:T(8,128)(2,1)S(1)}, bf16[1024,2048]{1,0:T(8,128)(2,1)S(1)}) custom-call(bf16[512,128]{1,0:T(8,128)(2,1)S(1)} %collective-permute-done.1.refs_0_, ...), custom_call_target="tpu_custom_call", output_to_operand_aliasing={{0}: (7, {}), {1}: (8, {}), {2}: (9, {}), {3}: (10, {})} | custom-call | flops 1000000000 | bytes 1000000 | tf_op jit(solution)/shard_map/pallas_call | solution.py:324
  24.6 0.0 collective-permute-done.got2
  24.6 0.0 collective-permute-done.3.got3
  24.6 2.5 %shard_map.107 = (bf16[2048,128]{1,0:T(8,128)(2,1)}, bf16[1024,128]{1,0:T(8,128)(2,1)}) custom-call(s32[1,1]{1,0:T(1,128)S(6)} %copy.21.live_ref, bf16[512,128]{1,0:T(8,128)(2,1)S(1)} %collective-permute-done.got2, bf16[512,128]{1,0:T(8,128)(2,1)S(1)} %collective-permute-done.3.got3, bf16[1024,2048]{1,0:T(8,128)(2,1)S(1)} %get-tuple-element.28.refs_3_.s_ref, ...), custom_call_target="tpu_custom_call" | custom-call | flops 1000000000 | bytes 1000000 | tf_op jit(solution)/shard_map/pallas_call | solution.py:334
  (1 shorter events, 0.0 us)
Async XLA Ops:
  5.5 14.9 %collective-permute-start.1 = (bf16[512,128]{1,0:T(8,128)(2,1)S(1)}, bf16[512,128]{1,0:T(8,128)(2,1)S(1)}, u32[]{:S(2)}, u32[]{:S(2)}) collective-permute-start(bf16[512,128]{1,0:T(8,128)(2,1)S(1)} %get-tuple-element.25), channel_id=1, source_target_pairs={{1,2},{3,4},{5,6},{7,8},{9,10},{11,12},{13,14},{2,1},{4,3},{6,5},{... | collective-permute-start | bytes 393224 | tf_op jit(solution)/shard_map/ppermute | solution.py:241
  7.5 12.9 %collective-permute-start.2 = (bf16[512,128]{1,0:T(8,128)(2,1)S(1)}, bf16[512,128]{1,0:T(8,128)(2,1)S(1)}, u32[]{:S(2)}, u32[]{:S(2)}) collective-permute-start(bf16[512,128]{1,0:T(8,128)(2,1)S(1)} %get-tuple-element.26), channel_id=1, source_target_pairs={{0,1},{2,3},{4,5},{6,7},{8,9},{10,11},{12,13},{14,15},{1,0},{3,2},... | collective-permute-start | bytes 393224 | tf_op jit(solution)/shard_map/ppermute | solution.py:241
  14.4 10.2 %collective-permute-start = (bf16[512,128]{1,0:T(8,128)(2,1)S(1)}, bf16[512,128]{1,0:T(8,128)(2,1)S(1)}, u32[]{:S(2)}, u32[]{:S(2)}) collective-permute-start(bf16[512,128]{1,0:T(8,128)(2,1)S(1)} %get-tuple-element.24), channel_id=1, source_target_pairs={{16,32},{48,64},{80,96},{112,128},{144,160},{176,192},{208,224},{2... | collective-permute-start | bytes 393224 | tf_op jit(solution)/shard_map/ppermute | solution.py:241
  20.4 4.2 %collective-permute-start.3 = (bf16[512,128]{1,0:T(8,128)(2,1)S(1)}, bf16[512,128]{1,0:T(8,128)(2,1)S(1)}, u32[]{:S(2)}, u32[]{:S(2)}) collective-permute-start(bf16[512,128]{1,0:T(8,128)(2,1)S(1)} %get-tuple-element.33), channel_id=1, source_target_pairs={{0,16},{32,48},{64,80},{96,112},{128,144},{160,176},{192,208},{224... | collective-permute-start | bytes 393224 | tf_op jit(solution)/shard_map/ppermute | solution.py:241
